TPU v7x, 32 devices: a whole 2x2x4 slice. The times are simulated.
32 devices in a mesh: dp: 8 (over z, y), tensor: 4 (over x, core).
Axes of the slice: x: 2, y: 2, z: 4, core: 2. Of those that a mesh axis runs over, the one named last changes fastest.
Arguments:
- tokens: bfloat16 [16384, 768], P(('dp', 'tensor')), may hold values from -6 to 6
- lengths: int32 [8, 8], P('dp'), may hold values from 0 to 1365, as said below
- cotangent: bfloat16 [16384, 768], P(('dp', 'tensor')), may hold values from -6 to 6
- ln1_gain: bfloat16 [768], P(('dp', 'tensor')), may hold values from 0.25 to 1.75
- ln1_bias: bfloat16 [768], P(('dp', 'tensor')), may hold values from -4 to 4
- w_qkv: bfloat16 [3, 768, 768], P(None, 'dp', 'tensor'), may hold values from -0.3125 to 0.3125
- b_qv: bfloat16 [2, 768], P(None, ('tensor', 'dp')), may hold values from -6 to 6
- w_out: bfloat16 [768, 768], P('tensor', 'dp'), may hold values from -0.875 to 0.875
- b_out: bfloat16 [768], P(('dp', 'tensor')), may hold values from -4 to 4
- ln2_gain: bfloat16 [768], P(('dp', 'tensor')), may hold values from 0.25 to 1.75
- ln2_bias: bfloat16 [768], P(('dp', 'tensor')), may hold values from -4 to 4
- w_fc1: bfloat16 [768, 3072], P('dp', 'tensor'), may hold values from -0.21875 to 0.21875
- b_fc1: bfloat16 [3072], P(('tensor', 'dp')), may hold values from -6 to 6
- w_fc2: bfloat16 [3072, 768], P('tensor', 'dp'), may hold values from -0.109375 to 0.109375
- b_fc2: bfloat16 [768], P(('dp', 'tensor')), may hold values from -4 to 4
Outputs:
- mixed: bfloat16 [16384, 768], P(('dp', 'tensor'))
- input_grad: bfloat16 [16384, 768], P(('dp', 'tensor'))
- grad_ln1_gain: float32 [768], P(('dp', 'tensor'))
- grad_ln1_bias: float32 [768], P(('dp', 'tensor'))
- grad_w_qkv: float32 [3, 768, 768], P(None, 'dp', 'tensor')
- grad_b_qv: float32 [2, 768], P(None, ('tensor', 'dp'))
- grad_w_out: float32 [768, 768], P('tensor', 'dp')
- grad_b_out: float32 [768], P(('dp', 'tensor'))
- grad_ln2_gain: float32 [768], P(('dp', 'tensor'))
- grad_ln2_bias: float32 [768], P(('dp', 'tensor'))
- grad_w_fc1: float32 [768, 3072], P('dp', 'tensor')
- grad_b_fc1: float32 [3072], P(('tensor', 'dp'))
- grad_w_fc2: float32 [3072, 768], P('tensor', 'dp')
- grad_b_fc2: float32 [768], P(('dp', 'tensor'))
Inputs may be any that keep to these rules, and one draw needn't show every extreme that they name: Each row holds the lengths of the 8 documents of one group in order and sums to 2048. Entry 4 is the row's longest document: longer than 1024, starting before slot 512 and reaching slot 1536. Other entries may be 0.
All inputs are finite; a program needn't handle non-finite values.
Results may differ from a plain program's by a relative error of at most 0.02.
Values may be sent and summed in bfloat16 or wider, within the bound.
A program may use at most 128 MiB of HBM per device.

v0:
```python
import jax
import jax.numpy as jnp
from jax import lax
from jax.sharding import PartitionSpec as P

HEAD_DIM = 64
SLOTS = 2048
QBLOCK = 512


EPS = 1e-05
NEG = -1e30


def cut_along(x, dim, count):
    before, after = (x.shape[:dim], x.shape[dim + 1 :])
    return jnp.moveaxis(x.reshape(*before, count, -1, *after), dim, 0)


def sent_and_summed(x, axis, dim):
    count = lax.axis_size(axis)
    blocks = lax.all_to_all(cut_along(x, dim, count), axis, 0, 0, tiled=True)
    return jnp.sum(blocks.astype(jnp.float32), axis=0)


def layer_norm(v, gain, shift):
    mean = jnp.mean(v, axis=-1, keepdims=True)
    centered = v - mean
    spread = jnp.mean(centered * centered, axis=-1, keepdims=True)
    return centered * lax.rsqrt(spread + EPS) * gain + shift


def matmul(left, right):
    return jnp.dot(left, right, preferred_element_type=jnp.float32)


def transpose_dot(left, right):
    return lax.dot_general(
        left, right, (((0,), (0,)), ((), ())), preferred_element_type=jnp.float32
    )


def dot_rows(left, right):
    return lax.dot_general(
        left, right, (((1,), (1,)), ((), ())), preferred_element_type=jnp.float32
    )


def rounded(v):
    return lax.optimization_barrier(v.astype(jnp.bfloat16)).astype(jnp.float32)


def gelu_exact(v):
    return jax.nn.gelu(v, approximate=False)


def doc_ids(lengths_row, total):
    ends = jnp.cumsum(lengths_row)
    places = jnp.arange(total, dtype=jnp.int32)
    return jnp.sum((ends[None, :] <= places[:, None]).astype(jnp.int32), axis=1)


def allowed_mask(start, base, segment, count):
    rows = start + jnp.arange(count, dtype=jnp.int32)
    qseg = lax.dynamic_slice_in_dim(segment, start, count, 0)
    places = base + jnp.arange(SLOTS, dtype=jnp.int32)
    return (places[None, :] <= rows[:, None]) & (segment[None, :] == qseg[:, None])


def head_forward(query, keys, values, segment):
    total = query.shape[0]
    count = total // QBLOCK

    def block(index):
        start = index * QBLOCK
        base = start // SLOTS * SLOTS
        qpart = lax.dynamic_slice_in_dim(query, start, QBLOCK, 0)
        scores = dot_rows(qpart, keys) * 0.125
        scores = jnp.where(allowed_mask(start, base, segment, QBLOCK), scores, NEG)
        top = jnp.max(scores, axis=1, keepdims=True)
        expd = jnp.exp(scores - top)
        summed = jnp.sum(expd, axis=1, keepdims=True)
        probs = (expd / summed).astype(jnp.bfloat16)
        return (matmul(probs, values), (top + jnp.log(summed))[:, 0])

    outs, logsum = lax.map(block, jnp.arange(count, dtype=jnp.int32))
    return (outs.reshape(total, -1), logsum.reshape(total))


def head_backward(query, keys, values, grad_out, logsum, segment):
    total = query.shape[0]
    count = total // QBLOCK

    def block(carry, index):
        grad_keys, grad_values = carry
        start = index * QBLOCK
        base = start // SLOTS * SLOTS
        qpart = lax.dynamic_slice_in_dim(query, start, QBLOCK, 0)
        gpart = lax.dynamic_slice_in_dim(grad_out, start, QBLOCK, 0)
        lpart = lax.dynamic_slice_in_dim(logsum, start, QBLOCK, 0)
        scores = dot_rows(qpart, keys) * 0.125
        scores = jnp.where(allowed_mask(start, base, segment, QBLOCK), scores, NEG)
        probs = jnp.exp(scores - lpart[:, None])
        value_part = grad_values + transpose_dot(probs.astype(jnp.bfloat16), gpart)
        grad_values = value_part
        grad_probs = dot_rows(gpart, values)
        inner = jnp.sum(probs * grad_probs, axis=1, keepdims=True)
        grad_scores = (probs * (grad_probs - inner) * 0.125).astype(jnp.bfloat16)
        grad_query = matmul(grad_scores, keys)
        key_part = grad_keys + transpose_dot(grad_scores, qpart)
        grad_keys = key_part
        return ((grad_keys, grad_values), grad_query)

    zeros = jnp.zeros((total, keys.shape[1]), jnp.float32)
    (grad_keys, grad_values), grad_query = lax.scan(
        block, (zeros, zeros), jnp.arange(count, dtype=jnp.int32)
    )
    return (grad_query.reshape(total, -1), grad_keys, grad_values)


def ff_forward(inputs, w_first, b_first, w_second):
    pres, hids, pieces = ([], [], [])
    pre = matmul(inputs, w_first) + b_first.astype(jnp.float32)
    hid = gelu_exact(pre).astype(jnp.bfloat16)
    pieces.append(rounded(matmul(hid, w_second)))
    pres.append(pre)
    hids.append(hid)
    return (pres, hids, pieces)


def ff_backward(inputs, grad_rows, w_first, w_second, pres, hids):
    first_grads, bias_grads, second_grads = ([], [], [])
    grad_hid = dot_rows(grad_rows, w_second)
    _, pull = jax.vjp(gelu_exact, pres[0])
    grad_pre = pull(grad_hid)[0].astype(jnp.bfloat16)
    second_grads.append(transpose_dot(hids[0], grad_rows))
    first_grads.append(transpose_dot(inputs, grad_pre))
    bias_grads.append(jnp.sum(grad_pre, axis=0, dtype=jnp.float32))
    grad_inputs = rounded(dot_rows(grad_pre, w_first))
    return (grad_inputs, first_grads[0], bias_grads[0], second_grads[0])


def collect(rows):
    return lax.all_gather(rows, "tensor", axis=0, tiled=True)


def spread(terms):
    return lax.psum_scatter(
        terms.astype(jnp.bfloat16), "tensor", scatter_dimension=0, tiled=True
    ).astype(jnp.float32)


def ff_collect(rows):
    return lax.all_gather(rows, "tensor", axis=0, tiled=True)


def ff_spread(terms):
    return lax.psum_scatter(
        terms.astype(jnp.bfloat16), "tensor", scatter_dimension=0, tiled=True
    ).astype(jnp.float32)


def local(
    tokens,
    lengths,
    cotangent,
    ln1_gain,
    ln1_bias,
    w_qkv,
    b_qv,
    w_out,
    b_out,
    ln2_gain,
    ln2_bias,
    w_fc1,
    b_fc1,
    w_fc2,
    b_fc2,
):
    segment = doc_ids(lengths[0], SLOTS)
    vectors = (
        lax.all_gather(ln1_gain, ("dp", "tensor"), axis=0, tiled=True),
        lax.all_gather(ln1_bias, ("dp", "tensor"), axis=0, tiled=True),
        lax.all_gather(b_out, ("dp", "tensor"), axis=0, tiled=True),
        lax.all_gather(ln2_gain, ("dp", "tensor"), axis=0, tiled=True),
        lax.all_gather(ln2_bias, ("dp", "tensor"), axis=0, tiled=True),
        lax.all_gather(b_fc2, ("dp", "tensor"), axis=0, tiled=True),
    )
    gain_one, bias_one, out_bias, gain_two, bias_two, ff_bias = [
        v.astype(jnp.float32) for v in vectors
    ]
    att_qkv, att_bias, att_out = (
        lax.all_gather(w_qkv, "dp", axis=1, tiled=True),
        lax.all_gather(b_qv, "dp", axis=1, tiled=True),
        lax.all_gather(w_out, "dp", axis=1, tiled=True),
    )
    ff_first, ff_mid_bias, ff_second = (
        lax.all_gather(w_fc1, "dp", axis=0, tiled=True),
        lax.all_gather(b_fc1, "dp", axis=0, tiled=True),
        lax.all_gather(w_fc2, "dp", axis=1, tiled=True),
    )
    inputs = tokens.astype(jnp.float32)
    whole_one = collect(layer_norm(inputs, gain_one, bias_one).astype(jnp.bfloat16))
    query = (matmul(whole_one, att_qkv[0]) + att_bias[0].astype(jnp.float32)).astype(jnp.bfloat16)
    keys = matmul(whole_one, att_qkv[1]).astype(jnp.bfloat16)
    values = (matmul(whole_one, att_qkv[2]) + att_bias[1].astype(jnp.float32)).astype(jnp.bfloat16)
    heads = query.shape[1] // HEAD_DIM
    outs, sums = ([], [])
    for head in range(heads):
        first = head * HEAD_DIM
        out_head, sum_head = head_forward(
            query[:, first : first + HEAD_DIM],
            keys[:, first : first + HEAD_DIM],
            values[:, first : first + HEAD_DIM],
            segment,
        )
        outs.append(out_head)
        sums.append(sum_head)
    attended = jnp.concatenate(outs, axis=1).astype(jnp.bfloat16)
    attn_rows = spread(matmul(attended, att_out))
    mid = inputs + attn_rows + out_bias
    low_two = layer_norm(mid, gain_two, bias_two).astype(jnp.bfloat16)
    whole_two = ff_collect(low_two)
    pres, hids, pieces = ff_forward(whole_two, ff_first, ff_mid_bias, ff_second)
    ff_rows = ff_spread(pieces[0])
    mixed = mid + ff_rows + ff_bias
    grad_out = cotangent.astype(jnp.float32)
    grad_ff_bias = jnp.sum(grad_out, axis=0)
    grad_low = grad_out.astype(jnp.bfloat16)
    grad_whole = ff_collect(grad_low)
    grad_partial, grad_first, grad_mid_bias, grad_second = ff_backward(
        whole_two, grad_whole, ff_first, ff_second, pres, hids
    )
    grad_two = ff_spread(grad_partial)
    _, pull_two = jax.vjp(layer_norm, mid, gain_two, bias_two)
    grad_mid_norm, grad_gain_two, grad_bias_two = pull_two(grad_two)
    grad_mid = grad_out + grad_mid_norm
    grad_out_bias = jnp.sum(grad_mid, axis=0)
    grad_rows = collect(grad_mid.astype(jnp.bfloat16))
    grad_attended = dot_rows(grad_rows, att_out).astype(jnp.bfloat16)
    grad_att_out = transpose_dot(attended, grad_rows)
    grads_query, grads_keys, grads_values = ([], [], [])
    for head in range(heads):
        first = head * HEAD_DIM
        grad_q, grad_k, grad_v = head_backward(
            query[:, first : first + HEAD_DIM],
            keys[:, first : first + HEAD_DIM],
            values[:, first : first + HEAD_DIM],
            grad_attended[:, first : first + HEAD_DIM],
            sums[head],
            segment,
        )
        grads_query.append(grad_q)
        grads_keys.append(grad_k)
        grads_values.append(grad_v)
    grad_query = jnp.concatenate(grads_query, axis=1).astype(jnp.bfloat16)
    grad_keys = jnp.concatenate(grads_keys, axis=1).astype(jnp.bfloat16)
    grad_values = jnp.concatenate(grads_values, axis=1).astype(jnp.bfloat16)
    grad_qkv = jnp.stack(
        [
            transpose_dot(whole_one, grad_query),
            transpose_dot(whole_one, grad_keys),
            transpose_dot(whole_one, grad_values),
        ],
        axis=0,
    )
    grad_bias_qv = jnp.stack(
        [
            jnp.sum(grad_query, axis=0, dtype=jnp.float32),
            jnp.sum(grad_values, axis=0, dtype=jnp.float32),
        ],
        axis=0,
    )
    grad_normed = (
        dot_rows(grad_query, att_qkv[0])
        + dot_rows(grad_keys, att_qkv[1])
        + dot_rows(grad_values, att_qkv[2])
    )
    grad_one = spread(grad_normed)
    _, pull_one = jax.vjp(layer_norm, inputs, gain_one, bias_one)
    grad_input_norm, grad_gain_one, grad_bias_one = pull_one(grad_one)
    grad_tokens = grad_mid + grad_input_norm
    att_grads = (
        sent_and_summed(grad_qkv.astype(jnp.bfloat16), "dp", 1),
        sent_and_summed(grad_bias_qv.astype(jnp.bfloat16), "dp", 1),
        sent_and_summed(grad_att_out.astype(jnp.bfloat16), "dp", 1),
    )
    ff_grads = (
        lax.psum_scatter(grad_first, "dp", scatter_dimension=0, tiled=True),
        lax.psum_scatter(grad_mid_bias, "dp", scatter_dimension=0, tiled=True),
        lax.psum_scatter(grad_second, "dp", scatter_dimension=1, tiled=True),
    )
    vec_grads = (
        lax.psum_scatter(grad_gain_one, ("dp", "tensor"), scatter_dimension=0, tiled=True),
        lax.psum_scatter(grad_bias_one, ("dp", "tensor"), scatter_dimension=0, tiled=True),
        lax.psum_scatter(grad_out_bias, ("dp", "tensor"), scatter_dimension=0, tiled=True),
        lax.psum_scatter(grad_gain_two, ("dp", "tensor"), scatter_dimension=0, tiled=True),
        lax.psum_scatter(grad_bias_two, ("dp", "tensor"), scatter_dimension=0, tiled=True),
        lax.psum_scatter(grad_ff_bias, ("dp", "tensor"), scatter_dimension=0, tiled=True),
    )
    return (
        mixed.astype(jnp.bfloat16),
        grad_tokens.astype(jnp.bfloat16),
        vec_grads[0],
        vec_grads[1],
        att_grads[0],
        att_grads[1],
        att_grads[2],
        vec_grads[2],
        vec_grads[3],
        vec_grads[4],
        ff_grads[0],
        ff_grads[1],
        ff_grads[2],
        vec_grads[5],
    )


def solution(mesh):
    in_specs = (
        P(("dp", "tensor"), None),
        P("dp", None),
        P(("dp", "tensor"), None),
        P(("dp", "tensor")),
        P(("dp", "tensor")),
        P(None, "dp", "tensor"),
        P(None, ("tensor", "dp")),
        P("tensor", "dp"),
        P(("dp", "tensor")),
        P(("dp", "tensor")),
        P(("dp", "tensor")),
        P("dp", "tensor"),
        P(("tensor", "dp")),
        P("tensor", "dp"),
        P(("dp", "tensor")),
    )
    out_specs = (
        P(("dp", "tensor"), None),
        P(("dp", "tensor"), None),
        P(("dp", "tensor")),
        P(("dp", "tensor")),
        P(None, "dp", "tensor"),
        P(None, ("tensor", "dp")),
        P("tensor", "dp"),
        P(("dp", "tensor")),
        P(("dp", "tensor")),
        P(("dp", "tensor")),
        P("dp", "tensor"),
        P(("tensor", "dp")),
        P("tensor", "dp"),
        P(("dp", "tensor")),
    )
    return jax.shard_map(local, mesh=mesh, in_specs=in_specs, out_specs=out_specs, check_vma=False)
```

profile of v0, /device:TPU:0, one launch (start us, length us, event | category | flops | bytes accessed | tf_op | source)
XLA Modules:
  0.0 974.4 jit_solution(13447828454761028721)
XLA Ops:
  13.1 42.2 %all-reduce.15 = (bf16[768]{0:T(1024)(128)(2,1)S(1)}, bf16[768]{0:T(1024)(128)(2,1)S(1)}, bf16[768]{0:T(1024)(128)(2,1)S(1)}, bf16[768]{0:T(1024)(128)(2,1)S(1)}...) all-reduce(bf16[768]{0:T(1024)(128)(2,1)S(1)} %dynamic-update-slice, ...), channel_id=1, replica_groups=mesh['dp'=8,'tensor'=4] {'dp','tensor'}, use_global_device_ids=true, to_apply=%add.4 | all-reduce | flops 4608 | bytes 18432
  61.7 20.5 %all-gather = bf16[8,24,2]{1,2,0:T(2,128)(2,1)S(1)} all-gather(bf16[1,24,2]{1,2,0:T(2,128)(2,1)S(1)} %bitcast.244), channel_id=1, replica_groups=mesh['dp'=8,'tensor'=4] {'dp'}, dimensions={0}, use_global_device_ids=true | all-gather | bytes 864 | tf_op jit(solution)/shard_map/all_gather | solution.py:194
  82.7 33.1 %all_gather.53 = bf16[192,768]{0,1:T(8,128)(2,1)} all-gather(bf16[192,96]{0,1:T(8,128)(2,1)S(1)} %copy.162), channel_id=1, replica_groups=mesh['dp'=8,'tensor'=4] {'dp'}, dimensions={1}, use_global_device_ids=true | all-gather | bytes 331776 | tf_op jit(solution)/shard_map/all_gather | solution.py:195
  115.9 36.3 %all_gather.51 = bf16[3,768,192]{2,1,0:T(8,128)(2,1)} all-gather(bf16[3,96,192]{2,1,0:T(8,128)(2,1)S(1)} %copy-done.54), channel_id=1, replica_groups=mesh['dp'=8,'tensor'=4] {'dp'}, dimensions={1}, use_global_device_ids=true | all-gather | bytes 995328 | tf_op jit(solution)/shard_map/all_gather | solution.py:193
  152.1 3.3 fusion.57
  160.8 3.1 convolution_convert_fusion.4
  165.0 37.6 %while.94 = (s32[]{:T(128)}, bf16[4,512,64]{1,2,0:T(8,128)(2,1)S(1)}, f32[4,512]{1,0:T(4,128)S(1)}, s32[4]{0:T(128)S(1)}, s32[2048]{0:T(1024)S(1)}, /*index=5*/b...) while((s32[]{:T(128)}, ...), condition=%wide.region_11.12_spmd, body=%wide.region_8.11_spmd.sunk | while | flops 279971840 | bytes 30464404 | solution.py:86
  171.4 3.2 fusion.203
  180.8 3.2 fusion.203
  190.1 3.2 fusion.203
  199.4 3.2 fusion.203
  204.4 33.7 %while.93 = (s32[]{:T(128)}, bf16[4,512,64]{1,2,0:T(8,128)(2,1)S(1)}, f32[4,512]{1,0:T(4,128)S(1)}, s32[4]{0:T(128)S(1)}, s32[2048]{0:T(1024)S(1)}, /*index=5*/b...) while((s32[]{:T(128)}, ...), condition=%wide.region_7.8_spmd, body=%wide.region_4.7_spmd.sunk | while | flops 279971840 | bytes 30726548 | solution.py:86
  209.6 3.2 fusion.198
  218.1 3.2 fusion.198
  226.5 3.2 fusion.198
  234.9 3.2 fusion.198
  241.7 40.2 %while.95 = (s32[]{:T(128)}, bf16[4,512,64]{1,2,0:T(8,128)(2,1)}, f32[4,512]{1,0:T(4,128)S(1)}, s32[4]{0:T(128)S(1)}, s32[2048]{0:T(1024)S(1)}, /*index=5*/bf16[...) while((s32[]{:T(128)}, bf16[4,512,64]{1,2,0:T(8,128)(2,1)}, ...), condition=%wide.region_15.16_spmd, body=%wide.region_12.15_spmd.sunk | while | flops 279971840 | bytes 32561612 | solution.py:86
  247.9 3.2 fusion.208
  257.9 3.2 fusion.208
  268.0 3.2 fusion.208
  278.0 3.2 fusion.208
  283.9 2.7 convolution_convert_fusion.2
  287.3 34.1 %reduce-scatter.7.cloned.1.call-done = bf16[512,768]{1,0:T(8,128)(2,1)} async-done(((bf16[2048,768]{1,0:T(8,128)(2,1)}), bf16[512,768]{1,0:T(8,128)(2,1)}) %reduce-scatter.7.cloned.1.call-update) | async-done | bytes 786448 | tf_op jit(solution)/shard_map/reduce_scatter | solution.py:148
  329.3 21.4 %all-reduce.5 = bf16[768]{0:T(1024)(128)(2,1)S(1)} all-reduce(bf16[768]{0:T(1024)(128)(2,1)S(1)} %dynamic-update-slice.5), channel_id=1, replica_groups=mesh['dp'=8,'tensor'=4] {'dp'}, use_global_device_ids=true, to_apply=%add.5 | all-reduce | flops 768 | bytes 3072
  350.7 6.0 all-gather.10.cloned.1.call-done
  356.6 7.5 fusion.96
  364.2 36.3 %all-gather.14.cloned.1.call-done = bf16[768,768]{0,1:T(8,128)(2,1)} async-done(((bf16[768,96]{0,1:T(8,128)(2,1)}), bf16[768,768]{0,1:T(8,128)(2,1)}) %all-gather.14.cloned.1.call-update) | async-done | bytes 1179664 | tf_op jit(solution)/shard_map/all_gather | solution.py:200
  400.5 28.5 %all-gather.16.cloned.1.call-done = bf16[2048,768]{1,0:T(8,128)(2,1)} async-done(((bf16[512,768]{1,0:T(8,128)(2,1)}), bf16[2048,768]{1,0:T(8,128)(2,1)}) %all-gather.16.cloned.1.call-update) | async-done | bytes 3145744 | tf_op jit(solution)/shard_map/all_gather | solution.py:154
  429.0 20.5 %convert_reduce_fusion = (f32[768]{0:T(1024)}, bf16[2048,768]{1,0:T(8,128)(2,1)S(1)}, f32[2048,768]{1,0:T(8,128)}) fusion(f32[2048,768]{1,0:T(8,128)} %fusion.96, f32[768]{0:T(1024)S(1)} %convert_element_type.193, bf16[2048,768]{1,0:T(8,128)(2,1)} %all-gather.16.cloned.1.call-done, bf16[768,768]{0,1:T(8,128)(2,1)} %all-gather.14.cloned.1.call-done), kind=kOutput, calls=%fused_computation.95 | convolution fusion | flops 2533883136 | bytes 20060160 | tf_op jit(solution)/shard_map/dot_general | solution.py:44
  451.3 4.0 convolution_convert_fusion
  455.3 5.6 multiply_convert_fusion.3
  462.6 4.0 convolution_convert_fusion.1
  467.3 26.1 %reduce-scatter.11.cloned.1.call-done = bf16[512,768]{1,0:T(8,128)(2,1)} async-done(((bf16[2048,768]{1,0:T(8,128)(2,1)}), bf16[512,768]{1,0:T(8,128)(2,1)}) %reduce-scatter.11.cloned.1.call-update) | async-done | bytes 786448 | tf_op jit(solution)/shard_map/reduce_scatter | solution.py:158
  495.9 2.8 fusion.73
  498.7 35.1 %reduce-scatter.9.cloned.1.call-done = bf16[512,768]{1,0:T(8,128)(2,1)} async-done(((bf16[2048,768]{1,0:T(8,128)(2,1)}), bf16[512,768]{1,0:T(8,128)(2,1)}) %reduce-scatter.9.cloned.1.call-update) | async-done | bytes 786448 | tf_op jit(solution)/shard_map/reduce_scatter | solution.py:158
  533.8 3.8 fusion.87
  540.1 28.2 %all-gather.18.cloned.1.call-done = bf16[2048,768]{1,0:T(8,128)(2,1)} async-done(((bf16[512,768]{1,0:T(8,128)(2,1)}), bf16[2048,768]{1,0:T(8,128)(2,1)}) %all-gather.18.cloned.1.call-update) | async-done | bytes 3145744 | tf_op jit(solution)/shard_map/all_gather | solution.py:144
  568.2 3.1 convolution_convert_fusion.3
  572.8 60.7 %while.98 = (s32[]{:T(128)}, f32[2048,64]{0,1:T(8,128)}, f32[2048,64]{0,1:T(8,128)}, bf16[4,512,64]{1,2,0:T(8,128)(2,1)}, s32[4]{0:T(128)S(1)}, /*index=5*/s32[2...) while((s32[]{:T(128)}, f32[2048,64]{0,1:T(8,128)}, ...), condition=%wide.region_31.32_spmd.clone, body=%wide.region_29.31_spmd.clone.sunk | while | flops 685246464 | bytes 73184336 | solution.py:115
  575.0 2.9 multiply_reduce_fusion.9
  589.9 2.9 multiply_reduce_fusion.9
  605.2 2.9 multiply_reduce_fusion.9
  620.5 2.9 multiply_reduce_fusion.9
  636.0 63.2 %while.97 = (s32[]{:T(128)}, f32[2048,64]{0,1:T(8,128)}, f32[2048,64]{0,1:T(8,128)}, bf16[4,512,64]{1,2,0:T(8,128)(2,1)}, s32[4]{0:T(128)S(1)}, /*index=5*/s32[2...) while((s32[]{:T(128)}, f32[2048,64]{0,1:T(8,128)}, ...), condition=%wide.region_28.29_spmd.clone, body=%wide.region_26.28_spmd.clone.sunk | while | flops 685246464 | bytes 69776376 | solution.py:115
  639.0 2.9 multiply_reduce_fusion.8
  654.5 2.9 multiply_reduce_fusion.8
  659.9 2.6 convolution_add_fusion.16
  670.4 2.9 multiply_reduce_fusion.8
  686.3 2.9 multiply_reduce_fusion.8
  701.7 56.0 %while.96 = (s32[]{:T(128)}, f32[2048,64]{0,1:T(8,128)}, f32[2048,64]{0,1:T(8,128)}, bf16[4,512,64]{1,2,0:T(8,128)(2,1)}, s32[4]{0:T(128)S(1)}, /*index=5*/s32[2...) while((s32[]{:T(128)}, f32[2048,64]{0,1:T(8,128)}, ...), condition=%wide.region_25.26_spmd.clone, body=%wide.region_23.25_spmd.clone.sunk | while | flops 685246464 | bytes 74232880 | solution.py:115
  703.9 2.9 multiply_reduce_fusion.7
  717.7 2.9 multiply_reduce_fusion.7
  731.7 2.9 multiply_reduce_fusion.7
  745.7 2.9 multiply_reduce_fusion.7
  765.5 2.8 add_convert_fusion
  768.3 7.1 fusion.97
  775.6 6.6 fusion.98
  785.7 5.6 all-to-all-start.1
  791.3 2.8 convolution_convert_fusion.6
  799.6 6.3 all-to-all-start.2
  822.1 6.0 all-to-all-start
  828.9 44.0 %all-reduce.12 = f32[768]{0:T(1024)} all-reduce(f32[768]{0:T(1024)} %get-tuple-element.1327), channel_id=12, replica_groups=mesh['dp'=8,'tensor'=4] {'dp'}, use_global_device_ids=true, to_apply=%region_52.53.clone | all-reduce | flops 768 | bytes 6144
  883.8 42.5 %all-reduce.14 = (f32[768]{0:T(1024)S(1)}, f32[768]{0:T(1024)S(1)}, f32[768]{0:T(1024)S(1)}, f32[768]{0:T(1024)S(1)}, f32[768]{0:T(1024)S(1)}, /*index=5*/f32[768]{0:T(1024)S(1)}) all-reduce(f32[768]{0:T(1024)S(1)} %get-tuple-element.1195, ...), channel_id=6, replica_groups=mesh['dp'=8,'tensor'=4] {'dp','tensor'}, use_global_device_ids=true, to_apply=%region_36.37.clone | all-reduce | flops 4608 | bytes 36864
  931.3 35.6 %reduce-scatter.17.cloned.1.call-done = f32[768,96]{0,1:T(8,128)} async-done(((f32[768,768]{0,1:T(8,128)}), f32[768,96]{0,1:T(8,128)}) %reduce-scatter.17.cloned.1.call-update) | async-done | bytes 294928 | tf_op jit(solution)/shard_map/reduce_scatter | solution.py:291
  (644 shorter events, 295.3 us)
Async XLA Ops:
  8.0 53.7 %copy-start.69 = (bf16[2,24]{1,0:T(2,128)(2,1)S(1)}, bf16[2,24]{1,0:T(2,128)(2,1)}, u32[]{:S(2)}) copy-start(bf16[2,24]{1,0:T(2,128)(2,1)} %param.33) | copy-start | bytes 292
  8.0 74.3 %copy-start.72 = (s32[1,8]{1,0:T(1,128)S(1)}, s32[1,8]{1,0:T(1,128)}, u32[]{:S(2)}) copy-start(s32[1,8]{1,0:T(1,128)} %param.28) | copy-start | bytes 100
  8.0 74.5 %copy-start.59 = (bf16[192,96]{1,0:T(8,128)(2,1)S(1)}, bf16[192,96]{1,0:T(8,128)(2,1)}, u32[]{:S(2)}) copy-start(bf16[192,96]{1,0:T(8,128)(2,1)} %param.34) | copy-start | bytes 110596
  8.0 107.8 %copy-start.54 = (bf16[3,96,192]{2,1,0:T(8,128)(2,1)S(1)}, bf16[3,96,192]{2,1,0:T(8,128)(2,1)}, u32[]{:S(2)}) copy-start(bf16[3,96,192]{2,1,0:T(8,128)(2,1)} %param.32) | copy-start | bytes 331780
  8.1 144.1 %all-gather.8.cloned.1.call-start = ((), (), s32[]{:S(2)}) async-start(), calls=%async_computation.9 | async-start | bytes 3932160 | tf_op jit(solution)/shard_map/all_gather | solution.py:144
  61.7 259.7 %reduce-scatter.7.cloned.1.call-start = ((), (), s32[]{:S(2)}) async-start(), calls=%async_computation.10 | async-start | bytes 3932160 | tf_op jit(solution)/shard_map/reduce_scatter | solution.py:148
  152.1 6.1 copy-start.29
  204.3 33.8 %copy-start.51 = (bf16[2048,64]{0,1:T(8,128)(2,1)S(1)}, bf16[2048,64]{0,1:T(8,128)(2,1)}, u32[]{:S(2)}) copy-start(bf16[2048,64]{0,1:T(8,128)(2,1)} %get-tuple-element.1355) | copy-start | bytes 786436
  241.7 42.2 %copy-start.38 = (bf16[192,768]{0,1:T(8,128)(2,1)S(1)}, bf16[192,768]{0,1:T(8,128)(2,1)}, u32[]{:S(2)}) copy-start(bf16[192,768]{0,1:T(8,128)(2,1)} %all_gather.53) | copy-start | bytes 884740
  283.9 37.5 %copy-start.6 = (bf16[512,768]{1,0:T(8,128)(2,1)S(1)}, bf16[512,768]{1,0:T(8,128)(2,1)}, u32[]{:S(2)}) copy-start(bf16[512,768]{1,0:T(8,128)(2,1)} %param.27) | copy-start | bytes 2359300
  286.6 64.0 %all-gather.12.cloned.1.call-start = ((), (), s32[]{:S(2)}) async-start(), calls=%async_computation.12 | async-start | bytes 1327104 | tf_op jit(solution)/shard_map/all_gather | solution.py:198
  287.2 69.4 %all-gather.10.cloned.1.call-start = ((), (), s32[]{:S(2)}) async-start(), calls=%async_computation.11 | async-start | bytes 3932160 | tf_op jit(solution)/shard_map/all_gather | solution.py:154
  323.0 6.1 copy-start.73
  325.9 74.6 %all-gather.14.cloned.1.call-start = ((), (), s32[]{:S(2)}) async-start(), calls=%async_computation.13 | async-start | bytes 1327104 | tf_op jit(solution)/shard_map/all_gather | solution.py:200
  326.5 102.5 %all-gather.16.cloned.1.call-start = ((), (), s32[]{:S(2)}) async-start(), calls=%async_computation.15 | async-start | bytes 3932160 | tf_op jit(solution)/shard_map/all_gather | solution.py:154
  327.3 166.2 %reduce-scatter.11.cloned.1.call-start = ((), (), s32[]{:S(2)}) async-start(), calls=%async_computation.16 | async-start | bytes 3932160 | tf_op jit(solution)/shard_map/reduce_scatter | solution.py:158
  429.0 22.2 %copy-start.70 = (bf16[768,768]{1,0:T(8,128)(2,1)S(1)}, bf16[768,768]{1,0:T(8,128)(2,1)}, u32[]{:S(2)}) copy-start(bf16[768,768]{1,0:T(8,128)(2,1)} %all-gather.12.cloned.1.call-done) | copy-start | bytes 3538948
  455.3 78.5 %reduce-scatter.9.cloned.1.call-start = ((), (), s32[]{:S(2)}) async-start(), calls=%async_computation.14 | async-start | bytes 3932160 | tf_op jit(solution)/shard_map/reduce_scatter | solution.py:158
  455.3 7.3 copy-start.71
  466.7 101.6 %all-gather.18.cloned.1.call-start = ((), (), s32[]{:S(2)}) async-start(), calls=%async_computation.17 | async-start | bytes 3932160 | tf_op jit(solution)/shard_map/all_gather | solution.py:144
  493.4 40.4 %copy-start.34 = (bf16[512,768]{1,0:T(8,128)(2,1)S(1)}, bf16[512,768]{1,0:T(8,128)(2,1)}, u32[]{:S(2)}) copy-start(bf16[512,768]{1,0:T(8,128)(2,1)} %reduce-scatter.11.cloned.1.call-done) | copy-start | bytes 2359300
  537.6 30.6 %copy-start.39 = (bf16[192,768]{0,1:T(8,128)(2,1)S(1)}, bf16[192,768]{0,1:T(8,128)(2,1)}, u32[]{:S(2)}) copy-start(bf16[192,768]{0,1:T(8,128)(2,1)} %all_gather.53) | copy-start | bytes 884740
  539.7 340.1 %reduce-scatter.13.cloned.1.call-start = ((), (), s32[]{:S(2)}) async-start(), calls=%async_computation.18 | async-start | bytes 3932160 | tf_op jit(solution)/shard_map/reduce_scatter | solution.py:148
  572.8 63.2 %copy-start.15 = (bf16[2048,64]{1,0:T(8,128)(2,1)S(1)}, bf16[2048,64]{1,0:T(8,128)(2,1)}, u32[]{:S(2)}) copy-start(bf16[2048,64]{1,0:T(8,128)(2,1)} %copy-done.14) | copy-start | bytes 786436
  572.8 5.1 copy-start.22
  572.8 5.1 copy-start.40
  580.4 4.9 copy-start.1
  587.6 5.2 copy-start.22
  587.6 5.2 copy-start.40
  595.3 5.1 copy-start.1
  602.9 5.2 copy-start.22
  602.9 5.2 copy-start.40
  610.6 5.1 copy-start.1
  618.2 5.2 copy-start.22
  618.2 5.2 copy-start.40
  625.9 5.1 copy-start.1
  636.0 65.7 %copy-start.13 = (bf16[2048,64]{1,0:T(8,128)(2,1)S(1)}, bf16[2048,64]{1,0:T(8,128)(2,1)}, u32[]{:S(2)}) copy-start(bf16[2048,64]{1,0:T(8,128)(2,1)} %copy-done.12) | copy-start | bytes 786436
  644.4 4.9 copy-start.3
  659.9 5.1 copy-start.3
  675.8 5.1 copy-start.3
  691.7 5.1 copy-start.3
  723.1 5.1 copy-start.16
  723.1 5.1 copy-start.5
  737.1 5.1 copy-start.16
  737.1 5.1 copy-start.5
  751.1 5.1 copy-start.16
  751.1 5.1 copy-start.5
  757.8 5.5 copy-start.35
  759.0 6.4 copy-start.47
  768.3 7.3 copy-start.43
  768.3 163.0 %reduce-scatter.15.cloned.1.call-start = ((), (), s32[]{:S(2)}) async-start(), calls=%async_computation.19 | async-start | bytes 2654208 | tf_op jit(solution)/shard_map/reduce_scatter | solution.py:289
  775.5 191.4 %reduce-scatter.17.cloned.1.call-start = ((), (), s32[]{:S(2)}) async-start(), calls=%async_computation.20 | async-start | bytes 2654208 | tf_op jit(solution)/shard_map/reduce_scatter | solution.py:291
  782.1 9.1 copy-start.30
  785.7 13.9 %all-to-all-start.1 = ((bf16[8,2,24]{2,1,0:T(2,128)(2,1)}), bf16[8,2,24]{2,1,0:T(2,128)(2,1)S(1)}, u32[]{:S(2)}, u32[]{:S(2)}) async-start(bf16[8,2,24]{2,1,0:T(2,128)(2,1)} %copy.182), calls=%async_computation.5 | async-start | bytes 8192 | tf_op jit(solution)/shard_map/all_to_all | solution.py:22
  799.6 8.8 copy-start.66
  799.6 22.5 %all-to-all-start.2 = ((bf16[8,192,96]{2,1,0:T(8,128)(2,1)}), bf16[8,192,96]{2,1,0:T(8,128)(2,1)}, u32[]{:S(2)}, u32[]{:S(2)}) async-start(bf16[8,192,96]{2,1,0:T(8,128)(2,1)} %bitcast.219), calls=%async_computation.6 | async-start | bytes 786432 | tf_op jit(solution)/shard_map/all_to_all | solution.py:22
  819.7 60.2 %copy-start.7 = (bf16[512,768]{1,0:T(8,128)(2,1)S(1)}, bf16[512,768]{1,0:T(8,128)(2,1)}, u32[]{:S(2)}) copy-start(bf16[512,768]{1,0:T(8,128)(2,1)} %param.27) | copy-start | bytes 2359300
  819.7 60.2 %copy-start.56 = (f32[768]{0:T(1024)S(1)}, f32[768]{0:T(1024)}, u32[]{:S(2)}) copy-start(f32[768]{0:T(1024)} %copy-done.55) | copy-start | bytes 9220
  819.7 60.2 %copy-start.58 = (f32[512]{0:T(512)S(1)}, f32[512]{0:T(512)}, u32[]{:S(2)}) copy-start(f32[512]{0:T(512)} %copy-done.57) | copy-start | bytes 6148
  822.1 59.6 %copy-start.65 = (f32[512]{0:T(512)S(1)}, f32[512]{0:T(512)}, u32[]{:S(2)}) copy-start(f32[512]{0:T(512)} %copy-done.64) | copy-start | bytes 6148
  822.1 59.6 %copy-start.61 = (f32[512]{0:T(512)S(1)}, f32[512]{0:T(512)}, u32[]{:S(2)}) copy-start(f32[512]{0:T(512)} %copy-done.60) | copy-start | bytes 6148
  822.1 55.0 %all-to-all-start = ((bf16[8,3,96,192]{2,3,1,0:T(8,128)(2,1)}), bf16[8,3,96,192]{2,3,1,0:T(8,128)(2,1)S(1)}, u32[]{:S(2)}, u32[]{:S(2)}) async-start(bf16[8,3,96,192]{2,3,1,0:T(8,128)(2,1)} %maximum_bitcast_fusion), calls=%async_computation.4 | async-start | bytes 2359296 | tf_op jit(solution)/shard_map/all_to_all | solution.py:22
  828.1 101.7 %copy-start.28 = (f32[512,768]{1,0:T(8,128)S(1)}, f32[512,768]{1,0:T(8,128)}, u32[]{:S(2)}) copy-start(f32[512,768]{1,0:T(8,128)} %copy-done.27) | copy-start | bytes 4718596
  879.9 49.9 %copy-start.33 = (bf16[512,768]{1,0:T(8,128)(2,1)S(1)}, bf16[512,768]{1,0:T(8,128)(2,1)}, u32[]{:S(2)}) copy-start(bf16[512,768]{1,0:T(8,128)(2,1)} %reduce-scatter.13.cloned.1.call-done) | copy-start | bytes 2359300
  (83 other events, 181.0 us)
Sparse Core Ops, SparseCore 0:
  61.8 28.7 all-gather.7
  286.7 34.6 reduce-scatter.6
  455.4 37.9 reduce-scatter.10
  495.8 37.9 reduce-scatter.8
Sparse Core Ops, SparseCore 1:
  289.5 38.1 all-gather.11
  329.8 26.8 all-gather.9
  358.9 41.5 all-gather.13
  402.2 26.8 all-gather.15
  539.8 28.3 all-gather.17
  768.3 37.8 reduce-scatter.12
  810.1 84.4 reduce-scatter.14
  898.5 68.3 reduce-scatter.16
where the time goes:
time: 984 us; the launch traced here: 974 us
  matrix products  266 us (27%)
  blocking collectives  240 us (24%)
  waiting for transfers between devices  232 us (24%)
  local copies, waits for them, and re-layouts  121 us (12%)
  other arithmetic  60 us (6%)
  starting transfers between devices  19 us (2%)
  loops' own time  18.3 us (2%)
  between operations  18.2 us (2%)
    unnamed x4, blocking collectives  150 us
    dot_general x42, matrix products, dot_rows(): lax.dot_general(left, right, (((1,), (1,)), ((), ())), preferred_element_...  101 us
    dot_general x30, matrix products, matmul(): return jnp.dot(left, right, preferred_element_type=jnp.float32)  89.9 us
    dot_general x30, matrix products, transpose_dot(): lax.dot_general(left, right, (((0,), (0,)), ((), ())), preferred_element_...  75.3 us
    reduce_scatter x2, waiting for transfers between devices, ff_spread(): lax.psum_scatter(terms.astype(jnp.bfloat16), 'tensor', scatter_dimension=...  61.2 us
    while x152, local copies, waits for them, and re-layouts  52.7 us
    all_gather x1, waiting for transfers between devices, local(): lax.all_gather(w_fc2, 'dp', axis=1, tiled=True)  36.3 us
    all_gather x1, blocking collectives, local(): lax.all_gather(w_qkv, 'dp', axis=1, tiled=True)  36.3 us
  transfers between devices with their start and end apart: 15, of which 8 were waited for; matrix products, arithmetic and copies ran while one was open for 9% of the time, Pallas kernels for 0%

commit v1 on v0

v1 whole, which is shorter than its diff:
```python
import jax
import jax.numpy as jnp
from jax import lax
from jax.sharding import PartitionSpec as P

HEAD_DIM = 64
SLOTS = 2048
BLOCK = 512
EPS = 1e-05
NEG = -1e30


def matmul(left, right):
    return jnp.dot(left, right, preferred_element_type=jnp.float32)


def transpose_dot(left, right):
    return lax.dot_general(
        left, right, (((0,), (0,)), ((), ())), preferred_element_type=jnp.float32
    )


def dot_rows(left, right):
    return lax.dot_general(
        left, right, (((1,), (1,)), ((), ())), preferred_element_type=jnp.float32
    )


def split_heads(x):
    total, width = x.shape
    return x.reshape(total, width // HEAD_DIM, HEAD_DIM).transpose(1, 0, 2)


def join_heads(x):
    return x.transpose(1, 0, 2).reshape(x.shape[1], -1)


def head_dot(spec, left, right):
    return jnp.einsum(spec, left, right, preferred_element_type=jnp.float32)


def masked_scores(query, keys, starts, begin):
    scores = head_dot("hqd,hkd->hqk", query, keys)
    rows = begin + lax.broadcasted_iota(jnp.int32, scores.shape[1:], 0)
    cols = lax.broadcasted_iota(jnp.int32, scores.shape[1:], 1)
    low = starts[begin : begin + BLOCK, None]
    return jnp.where(((cols >= low) & (cols <= rows))[None], scores, NEG)


def attend(starts, query, keys, values):
    outs, logs = [], []
    for begin in range(0, SLOTS, BLOCK):
        end = begin + BLOCK
        scores = masked_scores(query[:, begin:end], keys[:, :end], starts, begin)
        top = jnp.max(scores, axis=2, keepdims=True)
        weights = jnp.exp(scores - top)
        summed = jnp.sum(weights, axis=2, keepdims=True)
        out = head_dot("hqk,hkd->hqd", weights.astype(jnp.bfloat16), values[:, :end])
        outs.append((out / summed).astype(jnp.bfloat16))
        logs.append(top + jnp.log(summed))
    return jnp.concatenate(outs, axis=1), logs


def attend_back(starts, query, keys, values, grad, out, logs):
    inner = jnp.sum(grad.astype(jnp.float32) * out.astype(jnp.float32), axis=2, keepdims=True)
    grad_query, grad_keys, grad_values = [], 0.0, 0.0
    for step in reversed(range(SLOTS // BLOCK)):
        begin, end = step * BLOCK, (step + 1) * BLOCK
        q, g = query[:, begin:end], grad[:, begin:end]
        scores = masked_scores(q, keys[:, :end], starts, begin)
        probs = jnp.exp(scores - logs[step])
        dprobs = head_dot("hqd,hkd->hqk", g, values[:, :end])
        dscores = (probs * (dprobs - inner[:, begin:end])).astype(jnp.bfloat16)
        probs = probs.astype(jnp.bfloat16)
        grad_query.append(head_dot("hqk,hkd->hqd", dscores, keys[:, :end]) * 0.125)
        pad = ((0, 0), (0, SLOTS - end), (0, 0))
        grad_keys += jnp.pad(head_dot("hqk,hqd->hkd", dscores, q), pad)
        grad_values += jnp.pad(head_dot("hqk,hqd->hkd", probs, g), pad)
    grad_query = jnp.concatenate(grad_query[::-1], axis=1)
    parts = [join_heads(x.astype(jnp.bfloat16)) for x in (grad_query, grad_keys, grad_values)]
    return jnp.concatenate(parts, axis=1)


def feed(x, g, w1, b1, w2t):
    pre = matmul(x, w1) + b1
    half = 0.5 * (1.0 + lax.erf(pre * 0.7071067811865476))
    slope = half + pre * jnp.exp(-0.5 * pre * pre) * 0.3989422804014327
    hid = (pre * half).astype(jnp.bfloat16)
    hid, slope = lax.optimization_barrier((hid, slope))
    gp = (matmul(g, w2t) * slope).astype(jnp.bfloat16)
    gp = lax.optimization_barrier(gp)
    pieces = dot_rows(hid, w2t).astype(jnp.bfloat16)
    grad_pieces = dot_rows(gp, w1).astype(jnp.bfloat16)
    dw = jnp.concatenate(
        [transpose_dot(x, gp).astype(jnp.bfloat16), transpose_dot(g, hid).astype(jnp.bfloat16)],
        axis=1,
    )
    return pieces, grad_pieces, dw, jnp.sum(gp.astype(jnp.float32), axis=0)


FAR = [(t, t ^ 2) for t in range(4)]
PEER = [(t, t ^ 1) for t in range(4)]


def far(x):
    return lax.ppermute(x, "tensor", FAR)


def peer(x):
    return lax.ppermute(x, "tensor", PEER)


def gathered_pair(x):
    mine = jnp.stack([x, far(x)])
    return mine, peer(mine)


def gathered_mine_first(x):
    mine, theirs = gathered_pair(x)
    return jnp.concatenate([mine, theirs]).reshape(-1, x.shape[-1])


def gathered_in_order(x):
    mine, theirs = gathered_pair(x)
    index = lax.axis_index("tensor")
    chip, core = index // 2, index % 2
    near = jnp.where(core == 0, jnp.stack([mine, theirs], 1), jnp.stack([theirs, mine], 1))
    return jnp.where(chip == 0, near, near[::-1]).reshape(-1, x.shape[-1])


def summed_pair(keep, away):
    got = peer(away)
    other = (keep[1].astype(jnp.float32) + got[1].astype(jnp.float32)).astype(jnp.bfloat16)
    back = far(other)
    return keep[0].astype(jnp.float32) + got[0].astype(jnp.float32) + back.astype(jnp.float32)


def summed_mine_first(x):
    x = x.reshape(2, 2, -1, x.shape[-1])
    return summed_pair(x[0], x[1])


def summed_in_order(x):
    index = lax.axis_index("tensor")
    chip, core = index // 2, index % 2
    x = x.reshape(2, 2, -1, x.shape[-1])
    keep = lax.dynamic_index_in_dim(x, core, 1, keepdims=False)
    away = lax.dynamic_index_in_dim(x, 1 - core, 1, keepdims=False)
    return summed_pair(
        jnp.where(chip == 0, keep, keep[::-1]), jnp.where(chip == 0, away, away[::-1])
    )


def exchanged(x, axis):
    return lax.all_to_all(x, axis, 0, 0, tiled=True)


def spread_to_all(x, axis, count):
    return exchanged(jnp.broadcast_to(x[None], (count,) + x.shape), axis)


def summed_blocks(x, axis, count):
    blocks = exchanged(x.reshape(count, -1, x.shape[-1]), axis)
    return jnp.sum(blocks.astype(jnp.float32), axis=0)


def norm_parts(v):
    mean = jnp.mean(v, axis=-1, keepdims=True)
    centered = v - mean
    r = lax.rsqrt(jnp.mean(centered * centered, axis=-1, keepdims=True) + EPS)
    return centered * r, r


def norm_back(e, gain, vhat, r):
    u = e * gain
    return r * (
        u
        - jnp.mean(u, axis=-1, keepdims=True)
        - vhat * jnp.mean(u * vhat, axis=-1, keepdims=True)
    )


def local(
    tokens,
    lengths,
    cotangent,
    ln1_gain,
    ln1_bias,
    w_qkv,
    b_qv,
    w_out,
    b_out,
    ln2_gain,
    ln2_bias,
    w_fc1,
    b_fc1,
    w_fc2,
    b_fc2,
):
    n_dp = lax.axis_size("dp")
    n_tp = lax.axis_size("tensor")
    index = lax.axis_index("tensor")
    both = ("dp", "tensor")
    model = tokens.shape[1]
    width = w_out.shape[0]
    shard = model // n_dp
    piece_v = ln1_gain.shape[0]
    piece_b = b_qv.shape[1]
    piece_f = b_fc1.shape[0]

    ends = jnp.cumsum(lengths[0])
    places = jnp.arange(SLOTS, dtype=jnp.int32)
    starts = jnp.max(jnp.where(ends[None, :] <= places[:, None], ends[None, :], 0), axis=1)

    small = jnp.concatenate(
        [ln1_gain, ln1_bias, b_out, ln2_gain, ln2_bias, b_fc2, b_qv.reshape(-1), b_fc1]
    )
    small = jnp.pad(small, (0, -small.shape[0] % 128)).reshape(1, -1).astype(jnp.float32)
    small = spread_to_all(small, both, n_dp * n_tp)[:, 0]
    gain_one, bias_one, out_bias, gain_two, bias_two, ff_bias = [
        small[:, k * piece_v : (k + 1) * piece_v].reshape(-1) for k in range(6)
    ]
    group = lax.dynamic_index_in_dim(small.reshape(n_dp, n_tp, -1), index, 1, keepdims=False)
    at = 6 * piece_v
    b_query = group[:, at : at + piece_b].reshape(-1)
    b_value = group[:, at + piece_b : at + 2 * piece_b].reshape(-1)
    ff_mid_bias = group[:, at + 2 * piece_b : at + 2 * piece_b + piece_f].reshape(1, -1)
    qkv_bias = jnp.concatenate([b_query, jnp.zeros_like(b_query), b_value])

    qkv_shard = w_qkv.transpose(1, 0, 2).reshape(shard, 3 * width)
    att_qkv = spread_to_all(qkv_shard, "dp", n_dp).reshape(model, 3 * width)

    whole_tokens = gathered_in_order(tokens)
    out_rows = spread_to_all(w_out, "tensor", n_tp).reshape(model, shard)
    rest, _ = lax.optimization_barrier(
        (jnp.concatenate([out_rows.T, w_fc1, w_fc2.T], axis=1), att_qkv)
    )
    rest = lax.all_gather(rest, "dp", axis=0, tiled=True)
    att_out_t = rest[:, :model]
    hidden = w_fc1.shape[1]
    ff_first = rest[:, model : model + hidden]
    ff_second_t = rest[:, model + hidden :]

    vhat_all, _ = norm_parts(whole_tokens.astype(jnp.float32))
    whole_one = (vhat_all * gain_one + bias_one).astype(jnp.bfloat16)
    qkv = (matmul(whole_one, att_qkv) + qkv_bias).astype(jnp.bfloat16)
    cot_low, _ = lax.optimization_barrier((cotangent, qkv))
    grad_whole = gathered_mine_first(cot_low)

    query = split_heads(qkv[:, :width] * jnp.bfloat16(0.125))
    keys = split_heads(qkv[:, width : 2 * width])
    values = split_heads(qkv[:, 2 * width :])
    attended, lse = attend(starts, query, keys, values)
    rows = tokens.shape[0]
    heads_rows = exchanged(join_heads(attended).reshape(n_tp, rows, width), "tensor")
    heads_rows = jnp.moveaxis(heads_rows, 0, 1).reshape(rows, model)
    inputs = tokens.astype(jnp.float32)
    mid = inputs + dot_rows(heads_rows, att_out_t) + out_bias
    vhat_two, r_two = norm_parts(mid)
    low_two = (vhat_two * gain_two + bias_two).astype(jnp.bfloat16)
    whole_two = gathered_mine_first(low_two)

    pieces, grad_pieces, grad_ff, grad_mid_bias = feed(
        whole_two, grad_whole, ff_first, ff_mid_bias, ff_second_t
    )
    grad_two = summed_mine_first(grad_pieces)
    pieces, grad_ff, grad_two = lax.optimization_barrier((pieces, grad_ff, grad_two))
    grad_out = cotangent.astype(jnp.float32)
    grad_mid = grad_out + norm_back(grad_two, gain_two, vhat_two, r_two)
    grad_low = grad_mid.astype(jnp.bfloat16)
    grad_heads = matmul(grad_low, att_out_t).astype(jnp.bfloat16)
    grad_heads = jnp.moveaxis(grad_heads.reshape(rows, n_tp, width), 1, 0)
    grad_attended = exchanged(grad_heads, "tensor").reshape(-1, width)
    pieces, grad_ff, grad_attended = lax.optimization_barrier((pieces, grad_ff, grad_attended))

    mixed = mid + summed_mine_first(pieces) + ff_bias
    ff_sums = summed_blocks(grad_ff, "dp", n_dp)
    grad_out_t = transpose_dot(grad_low, heads_rows).astype(jnp.bfloat16)
    grad_out_t = jnp.moveaxis(grad_out_t.reshape(model, n_tp, width), 1, 0)
    grad_out_t = jnp.sum(exchanged(grad_out_t, "tensor").astype(jnp.float32), axis=0)

    grad_qkv = attend_back(
        starts, query, keys, values, split_heads(grad_attended), attended, lse
    )
    partial_one = dot_rows(grad_qkv, att_qkv)
    grad_one = summed_in_order(partial_one.astype(jnp.bfloat16))
    att_grads = jnp.concatenate(
        [transpose_dot(whole_one, grad_qkv).astype(jnp.bfloat16), grad_out_t.astype(jnp.bfloat16)],
        axis=1,
    )
    att_sums = summed_blocks(att_grads, "dp", n_dp)
    grad_qkv_w = att_sums[:, : 3 * width].reshape(shard, 3, width).transpose(1, 0, 2)
    grad_w_out = att_sums[:, 3 * width :].T

    grad_bias = jnp.sum(grad_qkv.astype(jnp.float32), axis=0)
    vectors = [
        jnp.sum(partial_one * vhat_all, axis=0),
        jnp.sum(partial_one, axis=0),
        jnp.sum(grad_mid, axis=0),
        jnp.sum(grad_two * vhat_two, axis=0),
        jnp.sum(grad_two, axis=0),
        jnp.sum(grad_out, axis=0),
    ]
    wide = jnp.stack([v.reshape(n_dp * n_tp, piece_v) for v in vectors], axis=1)
    wide = wide.reshape(n_dp, n_tp, 6 * piece_v)
    own = jnp.concatenate(
        [
            grad_bias[:width].reshape(n_dp, piece_b),
            grad_bias[2 * width :].reshape(n_dp, piece_b),
            grad_mid_bias.reshape(n_dp, piece_f),
        ],
        axis=1,
    )
    here = (jnp.arange(n_tp) == index)[None, :, None]
    own = jnp.where(here, own[:, None, :], 0.0)
    packed = jnp.concatenate([wide, own], axis=2)
    packed = jnp.pad(packed, ((0, 0), (0, 0), (0, -packed.shape[2] % 128)))
    sums = summed_blocks(packed.reshape(n_dp * n_tp, 1, -1), both, n_dp * n_tp)[0]
    vec = [sums[k * piece_v : (k + 1) * piece_v] for k in range(6)]
    grad_b_qv = sums[at : at + 2 * piece_b].reshape(2, piece_b)
    grad_b_fc1 = sums[at + 2 * piece_b : at + 2 * piece_b + piece_f]

    vhat_one, r_one = norm_parts(inputs)
    grad_tokens = grad_mid + norm_back(grad_one, gain_one, vhat_one, r_one)
    return (
        mixed.astype(jnp.bfloat16),
        grad_tokens.astype(jnp.bfloat16),
        vec[0],
        vec[1],
        grad_qkv_w,
        grad_b_qv,
        grad_w_out,
        vec[2],
        vec[3],
        vec[4],
        ff_sums[:, :hidden],
        grad_b_fc1,
        ff_sums[:, hidden:].T,
        vec[5],
    )


def solution(mesh):
    in_specs = (
        P(("dp", "tensor"), None),
        P("dp", None),
        P(("dp", "tensor"), None),
        P(("dp", "tensor")),
        P(("dp", "tensor")),
        P(None, "dp", "tensor"),
        P(None, ("tensor", "dp")),
        P("tensor", "dp"),
        P(("dp", "tensor")),
        P(("dp", "tensor")),
        P(("dp", "tensor")),
        P("dp", "tensor"),
        P(("tensor", "dp")),
        P("tensor", "dp"),
        P(("dp", "tensor")),
    )
    out_specs = (
        P(("dp", "tensor"), None),
        P(("dp", "tensor"), None),
        P(("dp", "tensor")),
        P(("dp", "tensor")),
        P(None, "dp", "tensor"),
        P(None, ("tensor", "dp")),
        P("tensor", "dp"),
        P(("dp", "tensor")),
        P(("dp", "tensor")),
        P(("dp", "tensor")),
        P("dp", "tensor"),
        P(("tensor", "dp")),
        P("tensor", "dp"),
        P(("dp", "tensor")),
    )
    return jax.shard_map(local, mesh=mesh, in_specs=in_specs, out_specs=out_specs, check_vma=False)
```

time: 984 us -> 438 us (0.45)
  blocking collectives: 240 us -> 0 us
  matrix products: 266 us -> 117 us
  waiting for transfers between devices: 232 us -> 129 us
  local copies, waits for them, and re-layouts: 121 us -> 46.9 us
  starting transfers between devices: 19 us -> 48.5 us
  loops' own time: 18.3 us -> 0 us
  other arithmetic: 60 us -> 76.3 us
    unnamed x4 -> x0, blocking collectives: 150 us -> none
    reduce_scatter x6 -> x0, waiting for transfers between devices: 131 us -> none  [the longest x2 61.2 us: ff_spread(): lax.psum_scatter(terms.astype(jnp.bfloat16), 'tensor', scatter_dimension=...]
    all_gather x6 -> x1, waiting for transfers between devices: 99 us -> 0.01 us  [local(): rest = lax.all_gather(rest, 'dp', axis=0, tiled=True)]
    all_gather x3 -> x0, blocking collectives: 89.9 us -> none  [the longest x1 36.3 us: local(): lax.all_gather(w_qkv, 'dp', axis=1, tiled=True)]
    dot_general x42 -> x4, matrix products: 101 us -> 18.2 us  [dot_rows(): lax.dot_general(left, right, (((1,), (1,)), ((), ())), preferred_element_...]
    ppermute x0 -> x12, waiting for transfers between devices: none -> 75.7 us  [the longest x6 75.5 us: far(): return lax.ppermute(x, 'tensor', FAR)]
    dot_general x30 -> x4, matrix products: 89.9 us -> 24.1 us  [matmul(): return jnp.dot(left, right, preferred_element_type=jnp.float32)]
    dot_general x30 -> x4, matrix products: 75.3 us -> 14.3 us  [transpose_dot(): lax.dot_general(left, right, (((0,), (0,)), ((), ())), preferred_element_...]
  transfers between devices with their start and end apart: 15 -> 22, of which waited for: 8 -> 12; matrix products, arithmetic and copies ran while one was open for 9% -> 45% of each run, Pallas kernels for 0% -> 0%
where the time goes in v1:
time: 438 us; the launch traced here: 434 us
  waiting for transfers between devices  129 us (29%)
  matrix products  117 us (27%)
  other arithmetic  76.3 us (17%)
  starting transfers between devices  48.5 us (11%)
  local copies, waits for them, and re-layouts  46.9 us (11%)
  between operations  15.6 us (4%)
    ppermute x6, waiting for transfers between devices, far(): return lax.ppermute(x, 'tensor', FAR)  75.5 us
    dot_general x24, matrix products, head_dot(): return jnp.einsum(spec, left, right, preferred_element_type=jnp.float32)  60.5 us
    all_to_all x9, waiting for transfers between devices, exchanged(): return lax.all_to_all(x, axis, 0, 0, tiled=True)  53.5 us
    all_to_all x9, starting transfers between devices, exchanged(): return lax.all_to_all(x, axis, 0, 0, tiled=True)  41.1 us
    dot_general x4, matrix products, matmul(): return jnp.dot(left, right, preferred_element_type=jnp.float32)  24.1 us
    dot_general x4, matrix products, dot_rows(): lax.dot_general(left, right, (((1,), (1,)), ((), ())), preferred_element_...  18.2 us
    dot_general x4, matrix products, transpose_dot(): lax.dot_general(left, right, (((0,), (0,)), ((), ())), preferred_element_...  14.3 us
    reduce_sum x4, other arithmetic, attend(): summed = jnp.sum(weights, axis=2, keepdims=True)  13.2 us
  transfers between devices with their start and end apart: 22, of which 12 were waited for; matrix products, arithmetic and copies ran while one was open for 45% of the time, Pallas kernels for 0%

profile of v1, /device:TPU:0, one launch (start us, length us, event | category | flops | bytes accessed | tf_op | source)
XLA Modules:
  0.0 433.6 jit_solution(8562792350863585242)
XLA Ops:
  8.0 4.8 %concatenate.39 = bf16[288]{0:T(512)(128)(2,1)S(1)} concatenate(bf16[24]{0:T(256)(128)(2,1)} %param.18, bf16[24]{0:T(256)(128)(2,1)} %param.19, bf16[24]{0:T(256)(128)(2,1)} %param.23, bf16[24]{0:T(256)(128)(2,1)} %param.24, bf16[24]{0:T(256)(128)(2,1)} %param.25, bf16[24]{0:T(256)(128)(2,1)} %param.29, bf16[48]{0:T(256)(128)(2,1)S(1)} %reshape.457, bf16[96]{0:T(256)(128)(2,1)} %param.27), dimensions={0} | concatenate | bytes 1152 | tf_op jit(solution)/shard_map/concatenate | solution.py:215
  13.4 7.3 %all-to-all-start = ((f32[32,1,384]{2,1,0:T(1,128)}), f32[32,1,384]{2,1,0:T(1,128)S(1)}, u32[]{:S(2)}, u32[]{:S(2)}) async-start(f32[32,1,384]{2,1,0:T(1,128)} %broadcast_in_dim.161), calls=%async_computation | async-start | bytes 98304 | tf_op jit(solution)/shard_map/all_to_all | solution.py:155
  28.8 3.4 all-to-all-start.3
  32.2 9.6 %collective-permute-done = bf16[512,768]{1,0:T(8,128)(2,1)S(1)} collective-permute-done((bf16[512,768]{1,0:T(8,128)(2,1)}, bf16[512,768]{1,0:T(8,128)(2,1)S(1)}, u32[]{:S(2)}, u32[]{:S(2)}) %collective-permute-start) | collective-permute-done | bytes 786464 | tf_op jit(solution)/shard_map/ppermute | solution.py:106
  44.7 5.5 %all-to-all-start.1 = ((bf16[8,96,576]{2,1,0:T(8,128)(2,1)}), bf16[8,96,576]{2,1,0:T(8,128)(2,1)}, u32[]{:S(2)}, u32[]{:S(2)}) async-start(bf16[8,96,576]{2,1,0:T(8,128)(2,1)} %broadcast_in_dim.163), calls=%async_computation.1 | async-start | bytes 1966080 | tf_op jit(solution)/shard_map/all_to_all | solution.py:155
  54.4 20.9 %all-to-all-done.1 = bf16[8,96,576]{2,1,0:T(8,128)(2,1)} async-done(((bf16[8,96,576]{2,1,0:T(8,128)(2,1)}), bf16[8,96,576]{2,1,0:T(8,128)(2,1)}, u32[]{:S(2)}, u32[]{:S(2)}) %all-to-all-start.1) | async-done | bytes 884768 | tf_op jit(solution)/shard_map/all_to_all | solution.py:155
  75.3 3.4 maximum_select_fusion
  83.5 3.3 add_convert_fusion.2
  89.0 1.9 fusion.19
  96.2 6.7 %select_reduce_fusion = (f32[3,512]{1,0:T(4,128)S(1)}, f32[3,512,2048]{2,1,0:T(8,128)}) fusion(pred[512,2048]{1,0:T(8,128)(4,1)S(1)} %fusion.30, bf16[3,2048,64]{1,2,0:T(8,128)(2,1)S(1)} %bitcast.188, bf16[3,2048,64]{1,2,0:T(8,128)(2,1)S(1)} %bitcast.198), kind=kOutput, calls=%fused_computation.6 | convolution fusion | flops 408943104 | bytes 14620672 | tf_op jit(solution)/shard_map/hqd,hkd->hqk/dot_general | solution.py:39
  102.9 2.8 fusion.3
  105.7 2.5 fusion.108
  108.3 7.8 %fusion = f32[3,512]{1,0:T(4,128)S(1)} fusion(f32[3,512,2048]{2,1,0:T(8,128)} %get-tuple-element.129, f32[3,512]{1,0:T(4,128)S(1)} %get-tuple-element.128, pred[512,2048]{1,0:T(8,128)(4,1)S(1)} %fusion.30), kind=kLoop, calls=%fused_computation.3 | loop fusion | flops 9435648 | bytes 13643776 | tf_op jit(solution)/shard_map/reduce_sum | solution.py:57
  116.2 6.3 %fusion.114 = bf16[3,512,64]{1,2,0:T(8,128)(2,1)S(1)} fusion(bf16[3,2048,64]{1,2,0:T(8,128)(2,1)S(1)} %bitcast.236, f32[3,512,2048]{2,1,0:T(8,128)} %get-tuple-element.129, f32[3,512]{1,0:T(4,128)S(1)} %get-tuple-element.128, pred[512,2048]{1,0:T(8,128)(4,1)S(1)} %fusion.30, f32[3,512]{1,0:T(4,128)S(1)} %fusion), kind=kOutput, calls=%fused_computation.167 | convolution fusion | flops 412286976 | bytes 14626816 | tf_op jit(solution)/shard_map/hqk,hkd->hqd/dot_general | solution.py:39
  124.9 4.0 all-to-all-start.2
  129.1 2.1 collective-permute-start.4
  131.2 9.8 %all-to-all-done.2 = bf16[4,512,192]{1,2,0:T(8,128)(2,1)S(1)} async-done(((bf16[4,512,192]{1,2,0:T(8,128)(2,1)}), bf16[4,512,192]{1,2,0:T(8,128)(2,1)S(1)}, u32[]{:S(2)}, u32[]{:S(2)}) %all-to-all-start.2) | async-done | bytes 786464 | tf_op jit(solution)/shard_map/all_to_all | solution.py:155
  141.9 2.4 fusion.182
  145.1 12.8 %collective-permute-done.4 = bf16[512,768]{1,0:T(8,128)(2,1)} collective-permute-done((bf16[512,768]{1,0:T(8,128)(2,1)}, bf16[512,768]{1,0:T(8,128)(2,1)}, u32[]{:S(2)}, u32[]{:S(2)}) %collective-permute-start.4) | collective-permute-done | bytes 786464 | tf_op jit(solution)/shard_map/ppermute | solution.py:106
  157.9 2.7 pad_maximum_fusion.6
  160.9 13.3 %collective-permute-done.2 = bf16[512,768]{1,0:T(8,128)(2,1)S(1)} collective-permute-done((bf16[512,768]{1,0:T(8,128)(2,1)S(1)}, bf16[512,768]{1,0:T(8,128)(2,1)S(1)}, u32[]{:S(2)}, u32[]{:S(2)}) %collective-permute-start.2) | collective-permute-done | bytes 786464 | tf_op jit(solution)/shard_map/ppermute | solution.py:106
  177.0 2.3 pad_maximum_fusion.1
  179.5 1.9 pad_maximum_fusion
  181.7 16.3 %fusion.9 = (f32[2048,768]{1,0:T(8,128)S(1)}, bf16[2048,768]{1,0:T(8,128)(2,1)S(1)}) fusion(f32[768]{0:T(1024)S(1)} %add.263, bf16[2048,768]{1,0:T(8,128)(2,1)S(1)} %bitcast.209, bf16[768,2304]{1,0:T(8,128)(2,1)S(1)} %copy-done.51), kind=kOutput, calls=%fused_computation.18 | convolution fusion | flops 2433220608 | bytes 13766656 | tf_op jit(solution)/shard_map/dot_general | solution.py:14
  198.0 2.8 multiply_convert_fusion.3
  200.9 3.1 convolution_convert_fusion
  205.2 2.8 convolution_convert_fusion.4
  208.0 2.8 convolution_convert_fusion.3
  213.0 4.0 convolution_convert_fusion.1
  217.0 13.6 %collective-permute-done.7 = bf16[512,768]{1,0:T(8,128)(2,1)S(1)} collective-permute-done((bf16[512,768]{1,0:T(8,128)(2,1)S(1)}, bf16[512,768]{1,0:T(8,128)(2,1)S(1)}, u32[]{:S(2)}, u32[]{:S(2)}) %collective-permute-start.7) | collective-permute-done | bytes 786464 | tf_op jit(solution)/shard_map/ppermute | solution.py:106
  236.4 2.3 copy.119
  238.7 4.2 all-to-all-start.4
  244.8 2.4 convert_reduce_fusion
  250.6 3.5 convolution_convert_fusion.2
  254.7 4.5 %all-to-all-start.6 = ((bf16[4,768,192]{1,2,0:T(8,128)(2,1)}), bf16[4,768,192]{1,2,0:T(8,128)(2,1)}, u32[]{:S(2)}, u32[]{:S(2)}) async-start(bf16[4,768,192]{1,2,0:T(8,128)(2,1)} %bitcast.203), calls=%async_computation.6 | async-start | bytes 2359296 | tf_op jit(solution)/shard_map/all_to_all | solution.py:155
  266.4 2.6 fusion.31
  269.0 2.4 multiply_convert_fusion.2
  274.8 3.3 fusion.22
  278.2 3.2 multiply_convert_fusion.1
  281.4 2.2 fusion.88
  284.8 5.8 %multiply_convert_fusion = bf16[3,512,2048]{2,1,0:T(8,128)(2,1)S(1)} fusion(f32[3,512,2048]{2,1,0:T(8,128)S(1)} %bitcast.180, f32[3,512]{1,0:T(4,128)S(1)} %get-tuple-element.107, f32[3,512]{1,0:T(4,128)S(1)} %copy-done.47, pred[512,2048]{1,0:T(8,128)(4,1)S(1)} %copy-done.5, bf16[3,2048,64]{1,2,0:T(8,128)(2,1)} %bitcast.237, bf16[3,2048,64]{1,2,0:T(8,128)(2,1)} %bitcast.222), kind=kOutput, calls=%fused_computation | convolution fusion | flops 418381824 | bytes 20918272 | tf_op jit(solution)/shard_map/hqd,hkd->hqk/dot_general | solution.py:39
  290.7 2.7 fusion.91
  293.4 5.8 %fusion.54 = bf16[3,2048,64]{1,2,0:T(8,128)(2,1)} fusion(f32[3,512,2048]{2,1,0:T(8,128)S(1)} %bitcast.180, f32[3,512]{1,0:T(4,128)S(1)} %copy-done.47, pred[512,2048]{1,0:T(8,128)(4,1)S(1)} %copy-done.5, f32[3,512,64]{1,2,0:T(8,128)} %fusion.70, f32[3,1024,64]{1,2,0:T(8,128)} %fusion.31, f32[3,1536,64]{1,2,0:T(8,128)} %fusion.22, ...), kind=kOutput, calls=%fused_computation.82 | convolution fusion | flops 413663232 | bytes 16979968 | tf_op jit(solution)/shard_map/hqk,hqd->hkd/dot_general | solution.py:39
  299.2 2.5 fusion.57
  303.3 8.7 %fusion.176 = (f32[768]{0:T(1024)S(1)}, f32[768]{0:T(1024)S(1)}, bf16[2048,768]{1,0:T(8,128)(2,1)}, bf16[2048,768]{1,0:T(8,128)(2,1)}) fusion(f32[2048]{0:T(1024)S(1)} %bitcast.254, f32[2048]{0:T(1024)S(1)} %bitcast.253, bf16[2,2,512,768]{3,2,1,0:T(8,128)(2,1)} %copy-done, pred[]{:T(512)S(6)} %eq.21, f32[768]{0:T(1024)S(1)} %add.246, f32[768]{0:T(1024)S(1)} %mul.190, ...), kind=kOutput, calls=%fused_computation.284 | convolution fusion | flops 1836317184 | bytes 12709889 | tf_op jit(solution)/shard_map/dot_general | solution.py:24
  313.4 5.3 %convolution_convert_fusion.5 = bf16[768,576]{0,1:T(8,128)(2,1)} fusion(bf16[2048,768]{1,0:T(8,128)(2,1)} %get-tuple-element.89, bf16[2048,192]{0,1:T(8,128)(2,1)} %bitcast.243, bf16[2048,192]{0,1:T(8,128)(2,1)S(1)} %bitcast.214, bf16[2048,192]{0,1:T(8,128)(2,1)} %bitcast.229), kind=kOutput, calls=%fused_computation.145 | convolution fusion | flops 1819459584 | bytes 6389760 | tf_op jit(solution)/shard_map/dot_general | solution.py:18
  318.7 4.3 %all-to-all-start.5 = ((f32[32,1,384]{2,1,0:T(1,128)}), f32[32,1,384]{2,1,0:T(1,128)}, u32[]{:S(2)}, u32[]{:S(2)}) async-start(f32[32,1,384]{2,1,0:T(1,128)} %reshape.490), calls=%async_computation.5 | async-start | bytes 98304 | tf_op jit(solution)/shard_map/all_to_all | solution.py:155
  323.1 2.2 reduce_sum.273
  328.1 2.3 all-to-all-done.5
  330.4 3.6 all-to-all-start.7
  334.0 3.2 dynamic-slice_bitcast_fusion.1
  338.8 4.3 copy.131
  343.1 20.0 %all-to-all-done.7 = bf16[8,96,768]{2,1,0:T(8,128)(2,1)S(1)} async-done(((bf16[8,96,768]{2,1,0:T(8,128)(2,1)}), bf16[8,96,768]{2,1,0:T(8,128)(2,1)S(1)}, u32[]{:S(2)}, u32[]{:S(2)}) %all-to-all-start.7) | async-done | bytes 1179680 | tf_op jit(solution)/shard_map/all_to_all | solution.py:155
  363.0 4.4 %all-to-all-start.8 = ((bf16[8,96,1536]{2,1,0:T(8,128)(2,1)}), bf16[8,96,1536]{2,1,0:T(8,128)(2,1)}, u32[]{:S(2)}, u32[]{:S(2)}) async-start(bf16[8,96,1536]{2,1,0:T(8,128)(2,1)} %bitcast.194), calls=%async_computation.8 | async-start | bytes 4718592 | tf_op jit(solution)/shard_map/all_to_all | solution.py:155
  367.6 2.7 slice.298
  371.4 3.5 reverse_select_fusion.2
  378.2 2.4 fusion.124
  383.7 2.4 fusion.74
  389.0 12.3 %collective-permute-done.11 = bf16[512,768]{1,0:T(8,128)(2,1)} collective-permute-done((bf16[512,768]{1,0:T(8,128)(2,1)}, bf16[512,768]{1,0:T(8,128)(2,1)}, u32[]{:S(2)}, u32[]{:S(2)}) %collective-permute-start.11) | collective-permute-done | bytes 786464 | tf_op jit(solution)/shard_map/ppermute | solution.py:106
  401.3 2.4 fusion.173
  403.7 14.1 %collective-permute-done.9 = bf16[512,768]{1,0:T(8,128)(2,1)} collective-permute-done((bf16[512,768]{1,0:T(8,128)(2,1)}, bf16[512,768]{1,0:T(8,128)(2,1)}, u32[]{:S(2)}, u32[]{:S(2)}) %collective-permute-start.9) | collective-permute-done | bytes 786464 | tf_op jit(solution)/shard_map/ppermute | solution.py:106
  417.8 2.9 fusion.78
  420.6 3.0 fusion.67
  423.7 2.0 convert_reduce_fusion.2
  (281 shorter events, 82.1 us)
Async XLA Ops:
  7.2 34.6 %copy-start.3 = (bf16[512,768]{1,0:T(8,128)(2,1)S(1)}, bf16[512,768]{1,0:T(8,128)(2,1)}, u32[]{:S(2)}) copy-start(bf16[512,768]{1,0:T(8,128)(2,1)} %param.15) | copy-start | bytes 2359300
  13.4 14.7 %all-to-all-start = ((f32[32,1,384]{2,1,0:T(1,128)}), f32[32,1,384]{2,1,0:T(1,128)S(1)}, u32[]{:S(2)}, u32[]{:S(2)}) async-start(f32[32,1,384]{2,1,0:T(1,128)} %broadcast_in_dim.161), calls=%async_computation | async-start | bytes 98304 | tf_op jit(solution)/shard_map/all_to_all | solution.py:155
  20.7 21.0 %collective-permute-start = (bf16[512,768]{1,0:T(8,128)(2,1)}, bf16[512,768]{1,0:T(8,128)(2,1)S(1)}, u32[]{:S(2)}, u32[]{:S(2)}) collective-permute-start(bf16[512,768]{1,0:T(8,128)(2,1)} %param.15), channel_id=1, source_target_pairs={{0,2},{1,3},{2,0},{3,1},{4,6},{5,7},{6,4},{7,5},{8,10},{9,11},{10,... | collective-permute-start | bytes 2359304 | tf_op jit(solution)/shard_map/ppermute | solution.py:106
  25.9 68.5 %copy-start.17 = (pred[512,1024]{1,0:T(8,128)(4,1)}, pred[512,1024]{1,0:T(8,128)(4,1)S(1)}, u32[]{:S(2)}) copy-start(pred[512,1024]{1,0:T(8,128)(4,1)S(1)} %fusion.58) | copy-start | bytes 1572868
  28.8 14.8 %all-to-all-start.3 = ((bf16[4,192,96]{1,2,0:T(8,128)(2,1)}), bf16[4,192,96]{1,2,0:T(8,128)(2,1)S(1)}, u32[]{:S(2)}, u32[]{:S(2)}) async-start(bf16[4,192,96]{1,2,0:T(8,128)(2,1)} %broadcast_in_dim.172), calls=%async_computation.3 | async-start | bytes 393216 | tf_op jit(solution)/shard_map/all_to_all | solution.py:155
  43.6 10.0 %copy-start.35 = (bf16[768,96]{0,1:T(8,128)(2,1)S(1)}, bf16[768,96]{0,1:T(8,128)(2,1)}, u32[]{:S(2)}) copy-start(bf16[768,96]{0,1:T(8,128)(2,1)} %param.28) | copy-start | bytes 442372
  43.6 10.0 %copy-start.36 = (bf16[96,768]{1,0:T(8,128)(2,1)S(1)}, bf16[96,768]{1,0:T(8,128)(2,1)}, u32[]{:S(2)}) copy-start(bf16[96,768]{1,0:T(8,128)(2,1)} %param.26) | copy-start | bytes 442372
  43.6 31.7 %collective-permute-start.1 = (bf16[2,512,768]{2,1,0:T(8,128)(2,1)}, bf16[2,512,768]{2,1,0:T(8,128)(2,1)}, u32[]{:S(2)}, u32[]{:S(2)}) collective-permute-start(bf16[2,512,768]{2,1,0:T(8,128)(2,1)} %get-tuple-element.96), channel_id=1, source_target_pairs={{0,1},{1,0},{2,3},{3,2},{4,5},{5,4},{6,7},{7,6},{8,9},{9,8},{10,11... | collective-permute-start | bytes 4718600 | tf_op jit(solution)/shard_map/ppermute | solution.py:110
  44.7 30.6 %all-to-all-start.1 = ((bf16[8,96,576]{2,1,0:T(8,128)(2,1)}), bf16[8,96,576]{2,1,0:T(8,128)(2,1)}, u32[]{:S(2)}, u32[]{:S(2)}) async-start(bf16[8,96,576]{2,1,0:T(8,128)(2,1)} %broadcast_in_dim.163), calls=%async_computation.1 | async-start | bytes 1966080 | tf_op jit(solution)/shard_map/all_to_all | solution.py:155
  50.1 90.8 %all-gather.2.cloned.1.call-start = ((), (), s32[]{:S(2)}) async-start(), calls=%async_computation.9 | async-start | bytes 3981312 | tf_op jit(solution)/shard_map/all_gather | solution.py:238
  51.8 64.3 %copy-start.4 = (pred[512,2048]{1,0:T(8,128)(4,1)}, pred[512,2048]{1,0:T(8,128)(4,1)S(1)}, u32[]{:S(2)}) copy-start(pred[512,2048]{1,0:T(8,128)(4,1)S(1)} %fusion.30) | copy-start | bytes 3145732
  78.8 3.1 copy-start
  87.0 9.2 %copy-start.11 = (bf16[2048,192]{0,1:T(8,128)(2,1)}, bf16[2048,192]{0,1:T(8,128)(2,1)S(1)}, u32[]{:S(2)}) copy-start(bf16[2048,192]{0,1:T(8,128)(2,1)S(1)} %get-tuple-element.92) | copy-start | bytes 2359300
  87.0 29.2 %copy-start.25 = (bf16[2048,192]{0,1:T(8,128)(2,1)}, bf16[2048,192]{0,1:T(8,128)(2,1)S(1)}, u32[]{:S(2)}) copy-start(bf16[2048,192]{0,1:T(8,128)(2,1)S(1)} %get-tuple-element.93) | copy-start | bytes 2359300
  87.7 3.8 copy-start.8
  89.0 5.4 %copy-start.2 = (f32[3,512,1024]{2,1,0:T(8,128)}, f32[3,512,1024]{2,1,0:T(8,128)S(1)}, u32[]{:S(2)}) copy-start(f32[3,512,1024]{2,1,0:T(8,128)S(1)} %get-tuple-element.135) | copy-start | bytes 18874372
  92.6 29.9 %copy-start.27 = (bf16[3,512,64]{1,2,0:T(8,128)(2,1)}, bf16[3,512,64]{1,2,0:T(8,128)(2,1)S(1)}, u32[]{:S(2)}) copy-start(bf16[3,512,64]{1,2,0:T(8,128)(2,1)S(1)} %fusion.95) | copy-start | bytes 589828
  94.4 11.3 %copy-start.1 = (f32[3,512,1536]{2,1,0:T(8,128)}, f32[3,512,1536]{2,1,0:T(8,128)S(1)}, u32[]{:S(2)}) copy-start(f32[3,512,1536]{2,1,0:T(8,128)S(1)} %get-tuple-element.133) | copy-start | bytes 28311556
  96.2 26.3 %copy-start.28 = (bf16[3,512,64]{1,2,0:T(8,128)(2,1)}, bf16[3,512,64]{1,2,0:T(8,128)(2,1)S(1)}, u32[]{:S(2)}) copy-start(bf16[3,512,64]{1,2,0:T(8,128)(2,1)S(1)} %fusion.102) | copy-start | bytes 589828
  108.3 14.3 %copy-start.29 = (bf16[3,512,64]{1,2,0:T(8,128)(2,1)}, bf16[3,512,64]{1,2,0:T(8,128)(2,1)S(1)}, u32[]{:S(2)}) copy-start(bf16[3,512,64]{1,2,0:T(8,128)(2,1)S(1)} %fusion.108) | copy-start | bytes 589828
  116.2 6.4 %copy-start.42 = (f32[3,512]{1,0:T(4,128)}, f32[3,512]{1,0:T(4,128)S(1)}, u32[]{:S(2)}) copy-start(f32[3,512]{1,0:T(4,128)S(1)} %fusion) | copy-start | bytes 18436
  124.9 16.1 %all-to-all-start.2 = ((bf16[4,512,192]{1,2,0:T(8,128)(2,1)}), bf16[4,512,192]{1,2,0:T(8,128)(2,1)S(1)}, u32[]{:S(2)}, u32[]{:S(2)}) async-start(bf16[4,512,192]{1,2,0:T(8,128)(2,1)} %copy.116), calls=%async_computation.2 | async-start | bytes 1572864 | tf_op jit(solution)/shard_map/all_to_all | solution.py:155
  129.1 28.8 %collective-permute-start.4 = (bf16[512,768]{1,0:T(8,128)(2,1)}, bf16[512,768]{1,0:T(8,128)(2,1)}, u32[]{:S(2)}, u32[]{:S(2)}) collective-permute-start(bf16[512,768]{1,0:T(8,128)(2,1)} %param.17), channel_id=1, source_target_pairs={{0,2},{1,3},{2,0},{3,1},{4,6},{5,7},{6,4},{7,5},{8,10},{9,11},{10,... | collective-permute-start | bytes 2359304 | tf_op jit(solution)/shard_map/ppermute | solution.py:106
  144.9 29.3 %collective-permute-start.2 = (bf16[512,768]{1,0:T(8,128)(2,1)S(1)}, bf16[512,768]{1,0:T(8,128)(2,1)S(1)}, u32[]{:S(2)}, u32[]{:S(2)}) collective-permute-start(bf16[512,768]{1,0:T(8,128)(2,1)S(1)} %add_convert_fusion.4), channel_id=1, source_target_pairs={{0,2},{1,3},{2,0},{3,1},{4,6},{5,7},{6,4},{7,5},{8,10},{9,11},{10,... | collective-permute-start | bytes 2359304 | tf_op jit(solution)/shard_map/ppermute | solution.py:106
  160.6 16.4 %collective-permute-start.5 = (bf16[2,512,768]{2,1,0:T(8,128)(2,1)}, bf16[2,512,768]{2,1,0:T(8,128)(2,1)}, u32[]{:S(2)}, u32[]{:S(2)}) collective-permute-start(bf16[2,512,768]{2,1,0:T(8,128)(2,1)} %pad_maximum_fusion.6), channel_id=1, source_target_pairs={{0,1},{1,0},{2,3},{3,2},{4,5},{5,4},{6,7},{7,6},{8,9},{9,8},{10,11... | collective-permute-start | bytes 4718600 | tf_op jit(solution)/shard_map/ppermute | solution.py:110
  160.9 13.3 %copy-start.15 = (bf16[1,512,768]{2,1,0:T(8,128)(2,1)}, bf16[1,512,768]{2,1,0:T(8,128)(2,1)S(1)}, u32[]{:S(2)}) copy-start(bf16[1,512,768]{2,1,0:T(8,128)(2,1)S(1)} %fusion.209) | copy-start | bytes 2359300
  175.7 3.8 collective-permute-start.3
  200.9 4.4 %copy-start.20 = (bf16[2048,768]{1,0:T(8,128)(2,1)}, bf16[2048,768]{1,0:T(8,128)(2,1)S(1)}, u32[]{:S(2)}) copy-start(bf16[2048,768]{1,0:T(8,128)(2,1)S(1)} %multiply_convert_fusion.3) | copy-start | bytes 9437188
  204.0 6.7 %collective-permute-start.6 = (bf16[2,512,768]{2,1,0:T(8,128)(2,1)S(1)}, bf16[2,512,768]{2,1,0:T(8,128)(2,1)S(1)}, u32[]{:S(2)}, u32[]{:S(2)}) collective-permute-start(bf16[2,512,768]{2,1,0:T(8,128)(2,1)S(1)} %bitcast.231), channel_id=1, source_target_pairs={{0,1},{1,0},{2,3},{3,2},{4,5},{5,4},{6,7},{7,6},{8,9},{9,8},{10,11... | collective-permute-start | bytes 4718600 | tf_op jit(solution)/shard_map/ppermute | solution.py:110
  211.0 19.5 %collective-permute-start.7 = (bf16[512,768]{1,0:T(8,128)(2,1)S(1)}, bf16[512,768]{1,0:T(8,128)(2,1)S(1)}, u32[]{:S(2)}, u32[]{:S(2)}) collective-permute-start(bf16[512,768]{1,0:T(8,128)(2,1)S(1)} %fusion.79), channel_id=1, source_target_pairs={{0,2},{1,3},{2,0},{3,1},{4,6},{5,7},{6,4},{7,5},{8,10},{9,11},{10,... | collective-permute-start | bytes 2359304 | tf_op jit(solution)/shard_map/ppermute | solution.py:106
  234.7 8.2 %copy-start.43 = (f32[3,512]{1,0:T(4,128)S(1)}, f32[3,512]{1,0:T(4,128)}, u32[]{:S(2)}) copy-start(f32[3,512]{1,0:T(4,128)} %copy-done.42) | copy-start | bytes 18436
  234.7 9.4 %copy-start.41 = (f32[2,4,2,128]{3,2,1,0:T(2,128)S(1)}, f32[2,4,2,128]{3,2,1,0:T(2,128)}, u32[]{:S(2)}) copy-start(f32[2,4,2,128]{3,2,1,0:T(2,128)} %get-tuple-element.114) | copy-start | bytes 24580
  238.7 15.9 %all-to-all-start.4 = ((bf16[4,512,192]{1,2,0:T(8,128)(2,1)}), bf16[4,512,192]{1,2,0:T(8,128)(2,1)}, u32[]{:S(2)}, u32[]{:S(2)}) async-start(bf16[4,512,192]{1,2,0:T(8,128)(2,1)} %bitcast.226), calls=%async_computation.4 | async-start | bytes 1572864 | tf_op jit(solution)/shard_map/all_to_all | solution.py:155
  254.7 64.1 %all-to-all-start.6 = ((bf16[4,768,192]{1,2,0:T(8,128)(2,1)}), bf16[4,768,192]{1,2,0:T(8,128)(2,1)}, u32[]{:S(2)}, u32[]{:S(2)}) async-start(bf16[4,768,192]{1,2,0:T(8,128)(2,1)} %bitcast.203), calls=%async_computation.6 | async-start | bytes 2359296 | tf_op jit(solution)/shard_map/all_to_all | solution.py:155
  259.2 3.2 copy-start.9
  260.6 17.6 %copy-start.21 = (bf16[4,24,8,512]{3,2,0,1:T(8,128)(2,1)}, bf16[4,24,8,512]{3,2,0,1:T(8,128)(2,1)S(1)}, u32[]{:S(2)}) copy-start(bf16[4,24,8,512]{3,2,0,1:T(8,128)(2,1)S(1)} %copy.144) | copy-start | bytes 2359300
  260.6 3.5 copy-start.26
  262.4 3.8 slice-start.6
  269.0 5.8 %slice-start.3 = ((s8[9437184]{0:T(1024)(128)(4,1)}), s8[4194304]{0:T(1024)(128)(4,1)S(1)}, s32[]{:S(2)}) async-start(s8[9437184]{0:T(1024)(128)(4,1)} %bitcast.181), calls=%async_computation.13 | async-start | bytes 8388608
  269.0 5.8 %slice-start.4 = ((s8[9437184]{0:T(1024)(128)(4,1)}), s8[4194304]{0:T(1024)(128)(4,1)S(1)}, s32[]{:S(2)}) async-start(s8[9437184]{0:T(1024)(128)(4,1)} %bitcast.181), calls=%async_computation.14 | async-start | bytes 8388608
  271.4 3.4 slice-start.5
  271.5 3.4 copy-start.14
  271.5 3.3 copy-start.46
  278.2 6.4 %slice-start = ((s8[12582912]{0:T(1024)(128)(4,1)}), s8[4194304]{0:T(1024)(128)(4,1)S(1)}, s32[]{:S(2)}) async-start(s8[12582912]{0:T(1024)(128)(4,1)} %bitcast.179), calls=%async_computation.10 | async-start | bytes 8388608
  278.2 6.4 %slice-start.1 = ((s8[12582912]{0:T(1024)(128)(4,1)}), s8[4194304]{0:T(1024)(128)(4,1)S(1)}, s32[]{:S(2)}) async-start(s8[12582912]{0:T(1024)(128)(4,1)} %bitcast.179), calls=%async_computation.11 | async-start | bytes 8388608
  281.4 3.2 slice-start.2
  299.2 2.5 copy-start.33
  299.2 2.5 copy-start.34
  299.2 3.5 copy-start.31
  303.3 9.0 %copy-start.39 = (f32[32,1,24]{2,0,1:T(8,128)S(1)}, f32[32,1,24]{2,0,1:T(8,128)}, u32[]{:S(2)}) copy-start(f32[32,1,24]{2,0,1:T(8,128)} %stack_reshape.20) | copy-start | bytes 9220
  303.3 9.0 %copy-start.38 = (f32[32,1,24]{2,0,1:T(8,128)S(1)}, f32[32,1,24]{2,0,1:T(8,128)}, u32[]{:S(2)}) copy-start(f32[32,1,24]{2,0,1:T(8,128)} %stack_reshape.21) | copy-start | bytes 9220
  303.3 9.0 %copy-start.40 = (f32[32,1,24]{2,0,1:T(8,128)S(1)}, f32[32,1,24]{2,0,1:T(8,128)}, u32[]{:S(2)}) copy-start(f32[32,1,24]{2,0,1:T(8,128)} %stack_reshape.22) | copy-start | bytes 9220
  303.3 9.0 %copy-start.37 = (f32[32,1,24]{2,0,1:T(8,128)S(1)}, f32[32,1,24]{2,0,1:T(8,128)}, u32[]{:S(2)}) copy-start(f32[32,1,24]{2,0,1:T(8,128)} %stack_reshape.23) | copy-start | bytes 9220
  303.3 9.2 %copy-start.44 = (f32[8,96]{1,0:T(8,128)S(1)}, f32[8,96]{1,0:T(8,128)}, u32[]{:S(2)}) copy-start(f32[8,96]{1,0:T(8,128)} %reshape.478) | copy-start | bytes 9220
  303.3 9.3 %copy-start.50 = (pred[4]{0:T(512)(128)(4,1)S(1)}, pred[4]{0:T(512)(128)(4,1)}, u32[]{:S(2)}) copy-start(pred[4]{0:T(512)(128)(4,1)} %iota_compare_fusion.10) | copy-start | bytes 16
  318.7 11.7 %all-to-all-start.5 = ((f32[32,1,384]{2,1,0:T(1,128)}), f32[32,1,384]{2,1,0:T(1,128)}, u32[]{:S(2)}, u32[]{:S(2)}) async-start(f32[32,1,384]{2,1,0:T(1,128)} %reshape.490), calls=%async_computation.5 | async-start | bytes 98304 | tf_op jit(solution)/shard_map/all_to_all | solution.py:155
  330.4 32.6 %all-to-all-start.7 = ((bf16[8,96,768]{2,1,0:T(8,128)(2,1)}), bf16[8,96,768]{2,1,0:T(8,128)(2,1)S(1)}, u32[]{:S(2)}, u32[]{:S(2)}) async-start(bf16[8,96,768]{2,1,0:T(8,128)(2,1)} %bitcast.204), calls=%async_computation.7 | async-start | bytes 2359296 | tf_op jit(solution)/shard_map/all_to_all | solution.py:155
  338.7 39.5 %collective-permute-start.10 = (bf16[2,512,768]{2,1,0:T(8,128)(2,1)}, bf16[2,512,768]{2,1,0:T(8,128)(2,1)}, u32[]{:S(2)}, u32[]{:S(2)}) collective-permute-start(bf16[2,512,768]{2,1,0:T(8,128)(2,1)} %reverse_select_fusion.1), channel_id=1, source_target_pairs={{0,1},{1,0},{2,3},{3,2},{4,5},{5,4},{6,7},{7,6},{8,9},{9,8},{10,11... | collective-permute-start | bytes 4718600 | tf_op jit(solution)/shard_map/ppermute | solution.py:110
  363.0 60.6 %all-to-all-start.8 = ((bf16[8,96,1536]{2,1,0:T(8,128)(2,1)}), bf16[8,96,1536]{2,1,0:T(8,128)(2,1)}, u32[]{:S(2)}, u32[]{:S(2)}) async-start(bf16[8,96,1536]{2,1,0:T(8,128)(2,1)} %bitcast.194), calls=%async_computation.8 | async-start | bytes 4718592 | tf_op jit(solution)/shard_map/all_to_all | solution.py:155
  370.3 13.5 %collective-permute-start.8 = (bf16[2,512,768]{2,1,0:T(8,128)(2,1)}, bf16[2,512,768]{2,1,0:T(8,128)(2,1)}, u32[]{:S(2)}, u32[]{:S(2)}) collective-permute-start(bf16[2,512,768]{2,1,0:T(8,128)(2,1)} %bitcast.35), channel_id=1, source_target_pairs={{0,1},{1,0},{2,3},{3,2},{4,5},{5,4},{6,7},{7,6},{8,9},{9,8},{10,11... | collective-permute-start | bytes 4718600 | tf_op jit(solution)/shard_map/ppermute | solution.py:110
  380.6 20.7 %collective-permute-start.11 = (bf16[512,768]{1,0:T(8,128)(2,1)}, bf16[512,768]{1,0:T(8,128)(2,1)}, u32[]{:S(2)}, u32[]{:S(2)}) collective-permute-start(bf16[512,768]{1,0:T(8,128)(2,1)} %fusion.124), channel_id=1, source_target_pairs={{0,2},{1,3},{2,0},{3,1},{4,6},{5,7},{6,4},{7,5},{8,10},{9,11},{10,... | collective-permute-start | bytes 2359304 | tf_op jit(solution)/shard_map/ppermute | solution.py:106
  386.2 31.6 %collective-permute-start.9 = (bf16[512,768]{1,0:T(8,128)(2,1)}, bf16[512,768]{1,0:T(8,128)(2,1)}, u32[]{:S(2)}, u32[]{:S(2)}) collective-permute-start(bf16[512,768]{1,0:T(8,128)(2,1)} %fusion.74), channel_id=1, source_target_pairs={{0,2},{1,3},{2,0},{3,1},{4,6},{5,7},{6,4},{7,5},{8,10},{9,11},{10,... | collective-permute-start | bytes 2359304 | tf_op jit(solution)/shard_map/ppermute | solution.py:106
  403.6 17.0 %copy-start.7 = (f32[512,768]{1,0:T(8,128)S(1)}, f32[512,768]{1,0:T(8,128)}, u32[]{:S(2)}) copy-start(f32[512,768]{1,0:T(8,128)} %copy-done.6) | copy-start | bytes 4718596
  403.7 17.0 %copy-start.10 = (bf16[2,512,768]{2,1,0:T(8,128)(2,1)S(1)}, bf16[2,512,768]{2,1,0:T(8,128)(2,1)}, u32[]{:S(2)}) copy-start(bf16[2,512,768]{2,1,0:T(8,128)(2,1)} %reverse_select_fusion.2) | copy-start | bytes 4718596
  (18 other events, 27.8 us)
Sparse Core Ops, SparseCore 0:
  75.4 64.2 all-gather.1
